TPU v7x, 32 devices: a whole 2x2x4 slice. The times are simulated.
32 devices in a mesh: tile: 16 (over z, y, core), dir: 2 (over x).
Axes of the slice: x: 2, y: 2, z: 4, core: 2. Of those that a mesh axis runs over, the one named last changes fastest.
Arguments:
- coherency: bfloat16 [32, 48, 12, 8, 256], P('tile', 'dir'), may hold values from -0.59765625 to 0.59765625
- observed: bfloat16 [32, 12, 8, 256], P('tile'), may hold values from -12 to 12
- flags: int32 [32, 3], P('tile'), may hold values 0 or 1
- tile_map: int32 [32, 2], P('tile'), may hold values from 0 to 31, as said below
- jones: float32 [48, 8, 512], P('dir', None, 'tile'), may hold values from -6 to 6
Outputs:
- residual: float32 [32, 12, 8, 256], P('tile', None, None, 'dir')
- gradient: float32 [48, 8, 512], P('dir', None, 'tile')
- curvature: float32 [48, 2, 512], P('dir', None, 'tile')
Inputs may be any that keep to these rules, and one draw needn't show every extreme that they name: `tile_map`: each row names a station block pair (row block, column block) with row block <= column block; no pair appears twice.
All inputs are finite; a program needn't handle non-finite values. No bound on the sum of `flags` on one device may be relied on, other than what follows from the above.
Results may differ from a plain program's by a relative error of at most 0.00035.
Values sent between devices are 32-bit elements; how exact they have to be, the bound alone decides.
No kernel may reach another device: no remote copies, remote signals or barrier semaphores. Data moves between devices by JAX's collectives and lax.ppermute only.
A program may use at most 64 MiB of HBM per device.

v0:
```python
import functools

import jax
import jax.numpy as jnp
from jax import lax
from jax.experimental import pallas as pl
from jax.experimental.pallas import tpu as pltpu
from jax.sharding import PartitionSpec as P

SB = 16
FREQ_CHANNELS = 4
LANES = 128
BASELINES = SB * SB
CHUNK = 3


def split_parts(values):
    shape = values.shape[:-2] + (2, 2, values.shape[-1])
    return (values[..., 0:4, :].reshape(shape), values[..., 4:8, :].reshape(shape))


def join_parts(re_part, im_part):
    shape = re_part.shape[:-3] + (4, re_part.shape[-1])
    return jnp.concatenate([re_part.reshape(shape), im_part.reshape(shape)], axis=-2)


def complex_product(left_re, left_im, right_re, right_im):
    lre = left_re[..., :, :, None, :]
    lim = left_im[..., :, :, None, :]
    rre = right_re[..., None, :, :, :]
    rim = right_im[..., None, :, :, :]
    return (jnp.sum(lre * rre - lim * rim, axis=-3), jnp.sum(lre * rim + lim * rre, axis=-3))


def adjoint(re_part, im_part):
    return (jnp.swapaxes(re_part, -3, -2), -jnp.swapaxes(im_part, -3, -2))


def weights(row_flag_mask, block_pair):
    valid_samples = jnp.repeat((1 - row_flag_mask).astype(jnp.float32), FREQ_CHANNELS)
    baseline = jnp.arange(SB * SB, dtype=jnp.int32)
    inner_row = baseline // SB
    inner_col = baseline % SB
    upper_triangle_pairs = jnp.where(
        (block_pair[0] < block_pair[1]) | (inner_row < inner_col), 1.0, 0.0
    ).astype(jnp.float32)
    return valid_samples[:, None, None] * upper_triangle_pairs[None, None, :]


def tile_terms(coher, jones_all, block_pair):
    row_gain_matrix = lax.dynamic_slice_in_dim(jones_all, block_pair[0] * SB, SB, 2)
    col_jones = lax.dynamic_slice_in_dim(jones_all, block_pair[1] * SB, SB, 2)
    first_antenna = jnp.repeat(row_gain_matrix, SB, axis=2)[:, None]
    station_q = jnp.tile(col_jones, (1, 1, SB))[:, None]
    coh_re, coh_im = split_parts(coher)
    p_re, p_im = split_parts(first_antenna)
    q_re, q_im = split_parts(station_q)
    qh_re, qh_im = adjoint(q_re, q_im)
    m_re, m_im = complex_product(coh_re, coh_im, qh_re, qh_im)
    n_re, n_im = complex_product(p_re, p_im, coh_re, coh_im)
    v_re, v_im = complex_product(p_re, p_im, m_re, m_im)
    predicted = jnp.sum(join_parts(v_re, v_im), axis=0)
    return (predicted, (m_re, m_im, n_re, n_im))


def station_terms(residual, weight, products):
    m_re, m_im, n_re, n_im = products
    r_re, r_im = split_parts(residual)
    mh_re, mh_im = adjoint(m_re, m_im)
    g_re, g_im = complex_product(r_re, r_im, mh_re, mh_im)
    row_side = jnp.sum(join_parts(g_re, g_im), axis=1)
    rh_re, rh_im = adjoint(r_re, r_im)
    f_re, f_im = complex_product(rh_re, rh_im, n_re, n_im)
    col_side = jnp.sum(join_parts(f_re, f_im), axis=1)
    row_curv = jnp.sum(jnp.sum(m_re * m_re + m_im * m_im, axis=-2) * weight[None], axis=1)
    column_curvature = jnp.sum(jnp.sum(n_re * n_re + n_im * n_im, axis=-3) * weight[None], axis=1)
    lead = row_side.shape[0]
    grad_row = jnp.sum(row_side.reshape(lead, 8, SB, SB), axis=3)
    grad_col = jnp.sum(col_side.reshape(lead, 8, SB, SB), axis=2)
    curv_row = jnp.sum(row_curv.reshape(lead, 2, SB, SB), axis=3)
    curv_col = jnp.sum(column_curvature.reshape(lead, 2, SB, SB), axis=2)
    return (grad_row, grad_col, curv_row, curv_col)


def add_block(total, piece, block):
    offset = block * SB
    current = lax.dynamic_slice_in_dim(total, offset, SB, 2)
    return lax.dynamic_update_slice_in_dim(total, current + piece, offset, 2)


def component(value):
    return lax.broadcasted_iota(jnp.int32, value.shape, value.ndim - 2)


def turn(value, ahead):
    return pltpu.roll(value, (8 - ahead) % 8, value.ndim - 2)


def flip(value, mask):
    if mask == 4:
        return turn(value, 4)
    return jnp.where(component(value) & mask == 0, turn(value, mask), turn(value, 8 - mask))


def transpose_matrix(value):
    place = component(value) & 3
    return jnp.where(place == 1, turn(value, 1), jnp.where(place == 2, turn(value, 7), value))


def fold(values):
    values = [values[x] + flip(values[x + 1], 1) for x in range(0, 4, 2)]
    return values[0] + flip(values[1], 2)


def pair_parts(first, second):
    low = component(first) < 4
    return jnp.where(low, first, turn(second, 4)), jnp.where(low, turn(first, 4), second)


def halves(value):
    high = value.astype(jnp.bfloat16)
    return high, (value - high.astype(jnp.float32)).astype(jnp.bfloat16)


def station_of(baseline, row_side):
    return baseline // SB if row_side else baseline % SB


def one_hot(row_side, transposed):
    shape = (BASELINES, LANES) if transposed else (LANES, BASELINES)
    lane = lax.broadcasted_iota(jnp.int32, shape, 1 if transposed else 0)
    baseline = lax.broadcasted_iota(jnp.int32, shape, 0 if transposed else 1)
    return (lane == station_of(baseline, row_side)).astype(jnp.bfloat16)


def expand(blocks, row_side):
    made = []
    for packed in blocks:
        made.extend([packed] + [pltpu.roll(packed, LANES - 2 * SB * g, 1) for g in range(1, 4)])
    high, low = halves(jnp.concatenate(made, axis=0))
    both = jnp.concatenate([high, low], axis=1)
    chosen = jnp.concatenate([one_hot(row_side, False)] * 2, axis=0)
    wide = jnp.dot(both, chosen, preferred_element_type=jnp.float32)
    ends = [0]
    for packed in blocks:
        ends.append(ends[-1] + 4 * packed.shape[0])
    return [wide[start:end] for start, end in zip(ends, ends[1:])]


def station_sums(values, row_side):
    high, low = halves(values)
    both = jnp.concatenate([high, low], axis=0)
    total = jnp.dot(both, one_hot(row_side, True), preferred_element_type=jnp.float32)
    count = high.shape[0]
    return total[:count] + total[count:]


def to_lanes(parts, half):
    moved = [pltpu.roll(part, 2 * SB * g + SB * half, 1) for g, part in enumerate(parts)]
    return sum(moved[1:], moved[0])


def arranged(ref, tile, half, k, mask):
    row = lambda c: ref[tile, half, pl.ds(8 * k + c, 8, stride=0), :]
    first = lax.broadcasted_iota(jnp.int32, (8, LANES), 0) & mask == 0
    pick = lambda c, d: jnp.where(first, row(c), row(d))
    return (pick(0, 3), pick(2, 1)), (pick(4, 7), pick(6, 5))


def half_lanes(index):
    return pl.ds(pl.multiple_of(index * LANES, LANES), LANES)


def upper_mask(meta, tile):
    shape = (8, BASELINES)
    baseline = lax.broadcasted_iota(jnp.int32, shape, 1)
    above = entry(meta, tile, 2, shape) < entry(meta, tile, 3, shape)
    return jnp.where((baseline // SB < baseline % SB) | above, 1.0, 0.0).astype(jnp.float32)


def pack_kernel(jones_in_hbm, slots, jones, packed, in_semaphore, semaphores):
    copy = pltpu.make_async_copy(jones_in_hbm, jones, in_semaphore)
    copy.start()
    copy.wait()
    each = jones.shape[0] // 4
    rows = packed.shape[0]
    packed[...] = jnp.concatenate(
        [jones[g * each : (g + 1) * each].reshape(rows, 2 * SB) for g in range(4)], axis=1
    )
    copies = [
        pltpu.make_async_copy(packed, slots.at[n], semaphores.at[n]) for n in range(slots.shape[0])
    ]
    for copy in copies:
        copy.start()
    for copy in copies:
        copy.wait()


def entry(meta, row, column, shape=(8, LANES)):
    return jnp.broadcast_to(meta[row : row + 1, column : column + 1], shape)


def station_block(meta, near, far, tile, side):
    block = entry(meta, tile, 2 + side)
    owner = block >> 1
    own_core = (owner ^ entry(meta, 0, 0)) & 1 == 0
    chips, rows = near.shape[:2]
    found = None
    for chip in range(chips):
        packed = jnp.where(own_core, near[chip].reshape(-1, 8, LANES), far[chip].reshape(-1, 8, LANES))
        found = packed if found is None else jnp.where(owner >> 1 == chip, packed, found)
    shifted = pltpu.roll(found.reshape(rows, LANES), LANES - SB, 1).reshape(found.shape)
    return jnp.where(block & 1 == 0, found, shifted).reshape(rows, LANES)


PIECES = 6


def block_of(meta, tile, side):
    return meta[tile, 2 + side]


def valid_of(flags, tile, sample):
    return (1 - flags[tile, sample // FREQ_CHANNELS]).astype(jnp.float32)


def sides(meta, tiles):
    return [[block_of(meta, tile, side) for tile in range(tiles)] for side in range(2)]


def pieces(source, target, semaphores):
    each = source.shape[0] // PIECES
    parts = [pl.ds(n * each, each) for n in range(PIECES)]
    return [
        pltpu.make_async_copy(source.at[part], target.at[part], semaphores.at[n])
        for n, part in enumerate(parts)
    ]


def moment_kernel(
    flags_in_hbm, source, moments_out, pairs,
    flags, coherency, moments, semaphores, flag_semaphore, out_semaphores,
):
    tiles, directions, samples = source.shape[:3]
    each = directions // PIECES
    flag_copy = pltpu.make_async_copy(flags_in_hbm, flags, flag_semaphore)
    flag_copy.start()
    copies = [pieces(source.at[t], coherency.at[t], semaphores.at[t]) for t in range(tiles)]
    for copy in sum(copies, []):
        copy.start()
    flag_copy.wait()
    sent = []
    for tile in range(tiles):

        def add_direction(k, _):
            rows = pl.ds(pl.multiple_of(8 * k, 8), 8)
            for half in range(2):
                lanes = slice(half * LANES, (half + 1) * LANES)
                sums = [jnp.zeros((8, LANES), jnp.float32)] * 4
                for s in range(samples):
                    c = coherency[tile, k, s, :, lanes].astype(jnp.float32)
                    weighted = valid_of(flags, tile, s) * c
                    sums = [v + weighted * (turn(c, n) if n else c) for n, v in enumerate(sums)]
                    if s % 2 == 1:
                        both = jnp.concatenate(pair_parts(before, c), axis=0)
                        pairs[tile, k, s // 2, :, lanes] = both.astype(pairs.dtype)
                    before = c
                for n in range(4):
                    moments[tile, n, rows, lanes] = sums[n]
            return 0

        for n, copy in enumerate(copies[tile]):
            copy.wait()
            lax.fori_loop(n * each, (n + 1) * each, add_direction, 0)
            rows = pl.ds(8 * n * each, 8 * each)
            sent.append(
                pltpu.make_async_copy(
                    moments.at[tile, :, rows],
                    moments_out.at[tile, :, rows],
                    out_semaphores.at[tile, n],
                )
            )
            sent[-1].start()
    for copy in sent:
        copy.wait()


def station_products(packed):
    e = packed.reshape(-1, 8, LANES)
    bits = component(e)
    part = bits >= 4
    second = bits & 1 != 0
    spread = lambda v: (lambda u: u + flip(u, 2))(v + flip(v, 4))
    across = flip(e, 1)
    squares = spread(e * e)
    cross_re = 2.0 * spread(e * across)
    sign = jnp.where(part == second, 1.0, -1.0)
    cross_im = 2.0 * spread(sign * (e * flip(across, 4)))
    made = jnp.where(bits & 2 == 0, squares, jnp.where(second, cross_im, cross_re))
    low = component(made[0]) < 4
    joined = [jnp.where(low, made[n], made[n + 1]) for n in range(0, made.shape[0], 2)]
    return jnp.concatenate(joined, axis=0)


def first_model_kernel(meta, near, far, narrow, model, row_jones, col_jones, paired, weight):
    tiles = narrow.shape[0]
    for side, jones in enumerate((row_jones, col_jones)):
        found = [station_block(meta, near, far, tile, side) for tile in range(tiles)]
        for tile, made in enumerate(expand(found, side == 0)):
            jones[tile, 0], jones[tile, 1] = made[:, :LANES], made[:, LANES:]
    models(0, narrow, row_jones, col_jones, model, paired, weight)


def next_model_kernel(tile, narrow, row_jones, col_jones, model, paired, weight):
    models(tile, narrow, row_jones, col_jones, model, paired, weight)


def models(tile, narrow, row_jones, col_jones, model, paired, weight):
    directions, pairs = paired.shape[:2]

    def weigh(k, _):
        for half in range(2):
            lanes = slice(half * LANES, (half + 1) * LANES)
            p_re, p_im = arranged(row_jones, tile, half, k, 2)
            q_re, q_im = arranged(col_jones, tile, half, k, 1)
            for x in range(4):
                a, b = x // 2, x % 2
                z_re = p_re[a] * q_re[b] + p_im[a] * q_im[b]
                z_im = p_im[a] * q_re[b] - p_re[a] * q_im[b]
                weight[k, 3 * x, :, lanes] = z_re
                weight[k, 3 * x + 1, :, lanes] = z_im - z_re
                weight[k, 3 * x + 2, :, lanes] = z_re + z_im
        return 0

    lax.fori_loop(0, directions, weigh, 0, unroll=2)

    def add_samples(step, _):
        lanes = half_lanes(step % 2)
        first = step // 2 * CHUNK
        zero = jnp.zeros((8, LANES), jnp.float32)
        low = component(zero) < 4
        sums = [[zero] * CHUNK for n in range(12)]
        for k in range(directions):
            parts = []
            for i in range(CHUNK):
                both = narrow[tile, k, first + i, :, lanes].astype(jnp.float32)
                real, imag = both[:8], both[8:]
                paired[k, first + i, 0, :, lanes] = real
                paired[k, first + i, 1, :, lanes] = imag
                parts.append((real + imag, real, imag))
            for n in range(12):
                w = weight[k, n, :, lanes]
                sums[n] = [sums[n][i] + w * parts[i][n % 3] for i in range(CHUNK)]
        for i in range(CHUNK):
            one, two, three = ([sums[3 * x + m][i] for x in range(4)] for m in range(3))
            real = fold([one[x] - three[x] for x in range(4)])
            imag = fold([one[x] + two[x] for x in range(4)])
            place = 2 * (first + i)
            model[place, :, lanes] = jnp.where(low, real, turn(imag, 4))
            model[place + 1, :, lanes] = jnp.where(low, turn(real, 4), imag)
        return 0

    lax.fori_loop(0, 2 * pairs // CHUNK, add_samples, 0)


def curvature_kernel(meta, near, far, moments, terms, masks, products):
    tiles = moments.shape[0]
    directions = moments.shape[2] // 8
    for tile in range(tiles):
        masks[tile, 0] = upper_mask(meta, tile)
        for time in range(masks.shape[1] - 1):
            valid = (1 - entry(meta, tile, 4 + time, (8, BASELINES))).astype(jnp.float32)
            masks[tile, 1 + time] = valid * masks[tile, 0]
    for side in range(2):
        found = [station_block(meta, near, far, tile, side) for tile in range(tiles)]
        made = expand([station_products(packed) for packed in found], side == 0)
        for tile in range(tiles):
            for half in range(2):
                products[tile, side, half] = made[tile][:, half * LANES : (half + 1) * LANES]

    def combine(step, _):
        tile, group = step // (directions // 4), step % (directions // 4)
        mask = masks[tile, 0]
        bits = component(mask[:, :LANES])
        odd = bits & 1 != 0
        upper = bits & 2 != 0
        sign = jnp.where(bits < 4, -1.0, 1.0)
        member = (bits >> 2) * 2 + (bits & 1)
        for half in range(2):
            lanes = slice(half * LANES, (half + 1) * LANES)
            found = [None, None]
            for i in range(4):
                k = 4 * group + i
                rows = pl.ds(pl.multiple_of(8 * k, 8), 8)
                m = [moments[tile, n, rows, lanes] for n in range(4)]
                row = lambda side, n: products[tile, side, half, pl.ds(4 * k + n, 8, stride=0), :]
                h = [row(1, n) for n in range(4)]
                row_sum = m[0] * jnp.where(odd, h[1], h[0])
                row_sum = row_sum + jnp.where(odd, sign * (m[3] * h[3]), m[1] * h[2])
                h = [row(0, n) for n in range(4)]
                col_sum = m[0] * jnp.where(upper, h[1], h[0])
                col_sum = col_sum + m[2] * jnp.where(upper, -sign * h[3], h[2])
                row_sum = row_sum + turn(row_sum, 4)
                row_sum = row_sum + flip(row_sum, 1)
                col_sum = transpose_matrix(col_sum)
                col_sum = col_sum + turn(col_sum, 4)
                col_sum = col_sum + flip(col_sum, 1)
                for side, v in enumerate((row_sum, col_sum)):
                    found[side] = v if i == 0 else jnp.where(member == i, v, found[side])
            for side in range(2):
                place = pl.ds(pl.multiple_of(8 * group, 8), 8)
                terms[side, tile, place, lanes] = mask[:, lanes] * found[side]
        return 0

    lax.fori_loop(0, tiles * directions // 4, combine, 0)


def add_to_owner(meta, near, far, block, part):
    owner = block // 2
    own_core = jnp.where(owner % 2 == meta[0, 0] % 2, 1.0, 0.0)
    near[owner // 2] = near[owner // 2] + own_core * part
    far[owner // 2] = far[owner // 2] + (1.0 - own_core) * part


def add_gradient_terms(
    tile, meta, masks, observed, mine, other, row_jones, col_jones, paired,
    residual_out, terms, residual, turned, semaphore,
):
    directions, pairs = paired.shape[:2]
    first_half = entry(meta, 0, 1) == 0
    for i in range(pairs):
        both = []
        for s in (2 * i, 2 * i + 1):
            summed = mine[s] + other[s]
            weight = masks[tile, 1 + s // FREQ_CHANNELS]
            r = weight * (observed[tile, s].astype(jnp.float32) - summed)
            residual[s] = jnp.where(first_half, r[:, :LANES], r[:, LANES:])
            both.append(r)
        made = [pair_parts(*both)]
        for x in range(1, 4):
            bit = x & -x
            made.append(tuple(flip(v, bit) for v in made[x - bit]))
        for x, (real, imag) in enumerate(made):
            turned[i, 3 * x] = real
            turned[i, 3 * x + 1] = real + imag
            turned[i, 3 * x + 2] = real - imag
    sent = pltpu.make_async_copy(residual, residual_out.at[tile], semaphore)
    sent.start()

    def add_directions(step, _):
        half, lanes = step % 2, half_lanes(step % 2)
        first = step // 2 * CHUNK
        zero = jnp.zeros((8, LANES), jnp.float32)
        sums = [[zero] * CHUNK for n in range(12)]
        for p in range(pairs):
            parts = []
            for i in range(CHUNK):
                real = paired[first + i, p, 0, :, lanes]
                imag = paired[first + i, p, 1, :, lanes]
                parts.append((real + imag, real, imag))
            for n in range(12):
                r = turned[p, n, :, lanes]
                sums[n] = [sums[n][i] + r * parts[i][n % 3] for i in range(CHUNK)]
        bits = component(zero)
        real = bits < 4
        equal = (bits >> 1) & 1 == bits & 1
        for i in range(CHUNK):
            k = first + i
            p_re, p_im = arranged(row_jones, tile, half, k, 2)
            q_re, q_im = arranged(col_jones, tile, half, k, 1)
            row_sum = [zero, zero]
            col_sum = [zero, zero]
            for x in range(4):
                a, b = x // 2, x % 2
                y_re = sums[3 * x][i] - sums[3 * x + 2][i]
                y_im = sums[3 * x + 1][i] - sums[3 * x][i]
                y_re = y_re + turn(y_re, 4)
                y_im = y_im + turn(y_im, 4)
                one, two = jnp.where(real, y_re, y_im), jnp.where(real, -y_im, y_re)
                row_sum[a] = row_sum[a] + (q_re[b] * one + q_im[b] * two)
                col_sum[b] = col_sum[b] + (p_re[a] * one - p_im[a] * two)
            rows = pl.ds(pl.multiple_of(8 * k, 8), 8)
            g, h = row_sum
            g = jnp.where(equal, g, h) + flip(jnp.where(equal, h, g), 1)
            terms[0, rows, lanes] = g
            g, h = col_sum
            g = jnp.where(equal, g, h) + flip(jnp.where(equal, h, g), 2)
            terms[1, rows, lanes] = g
        return 0

    lax.fori_loop(0, 2 * directions // CHUNK, add_directions, 0)
    return sent


def first_gradient_kernel(
    meta, masks, observed, mine, other, row_jones, col_jones, paired,
    residual_out, terms, residual, turned, semaphore,
):
    sent = add_gradient_terms(
        0, meta, masks, observed, mine, other, row_jones, col_jones, paired,
        residual_out, terms, residual, turned, semaphore,
    )
    sent.wait()


def last_gradient_kernel(
    tiles, meta_in_vmem, first_terms, curvature_terms,
    masks, observed, mine, other, row_jones, col_jones, paired,
    residual_before, residual_out, near, far, terms, residual, turned, semaphore,
    meta, meta_semaphore,
):
    del residual_before
    meta_copy = pltpu.make_async_copy(meta_in_vmem, meta, meta_semaphore)
    meta_copy.start()
    sent = add_gradient_terms(
        tiles - 1, meta_in_vmem, masks, observed, mine, other, row_jones, col_jones, paired,
        residual_out, terms, residual, turned, semaphore,
    )
    near[...] = jnp.zeros_like(near)
    far[...] = jnp.zeros_like(far)
    meta_copy.wait()
    directions = paired.shape[0]
    rows, few = 8 * directions, 2 * directions
    for side, blocks in enumerate(sides(meta, tiles)):
        stack = [first_terms[side], terms[side]]
        stack.extend(curvature_terms[side, tile] for tile in range(tiles))
        sums = station_sums(jnp.concatenate(stack, axis=0), side == 0)
        for tile, block in enumerate(blocks):
            half = block % 2
            part = to_lanes(jnp.split(sums[tile * rows : (tile + 1) * rows], 4, axis=0), half)
            part = part.reshape(-1, 8, LANES)
            if side == 0:
                part = transpose_matrix(part)
            else:
                part = jnp.where(component(part) < 4, part, -part)
            start = tiles * rows + tile * few
            groups = jnp.split(sums[start : start + few], directions // 4, axis=0)
            chosen = [groups[n : n + 4] for n in range(0, len(groups), 4)]
            made = [part.reshape(-1, LANES), *(to_lanes(parts, half) for parts in chosen)]
            add_to_owner(meta, near, far, block, jnp.concatenate(made, axis=0))
    sent.wait()


def finish_kernel(normalizer, parts, gradient, curvature):
    total = sum((parts[x] for x in range(1, parts.shape[0])), parts[0]) * normalizer
    directions = gradient.shape[0]
    rows, each = 2 * directions, directions // 4
    grad = total[:rows].reshape(each, 8, LANES)
    for g in range(4):
        gradient[g * each : (g + 1) * each] = grad[:, :, 2 * SB * g : 2 * SB * (g + 1)]
    for k in range(directions):
        group, member = k // 4, k % 4
        start = rows + group // 4 * 8 + member // 2 * 4 + member % 2
        lane = group % 4 * 2 * SB
        for c in range(2):
            row = total[start + 2 * c : start + 2 * c + 1]
            curvature[k, c : c + 1] = row[:, lane : lane + 2 * SB]


def call(kernel, scalars, arrays, in_hbm, results, scratch=(), to_hbm=(), aliases=None, cost=None):
    place = lambda space: pl.BlockSpec(memory_space=space)
    spaces = [pltpu.SMEM] * len(scalars) + [pltpu.VMEM] * len(arrays) + [pltpu.HBM] * len(in_hbm)
    return pl.pallas_call(
        kernel,
        in_specs=[place(space) for space in spaces],
        out_specs=[place(pltpu.HBM)] * len(to_hbm) + [place(pltpu.VMEM)] * len(results),
        out_shape=[
            *(pltpu.HBM(shape, jnp.float32) for shape in to_hbm),
            *(pltpu.VMEM(getattr(v, "shape", v), getattr(v, "dtype", jnp.float32)) for v in results),
        ],
        scratch_shapes=list(scratch),
        input_output_aliases=aliases or {},
        cost_estimate=cost,
        compiler_params=pltpu.CompilerParams(vmem_limit_bytes=32 * 1024 * 1024),
    )(*scalars, *arrays, *(pltpu.with_memory_space_constraint(v, pltpu.HBM) for v in in_hbm))


def swap_with(value, axis, mask):
    size = lax.axis_size(axis)
    return lax.ppermute(value, axis, [(place, place ^ mask) for place in range(size)])


def trade(slots):
    size = lax.axis_size("tile")
    groups = [list(range(core, size, 2)) for core in range(2)]
    return lax.all_to_all(slots, "tile", 0, 0, axis_index_groups=groups, tiled=True)


def body_kernels(coherency, observed, flags, tile_map, jones):
    tiles, directions, samples = coherency.shape[:3]
    chips = lax.axis_size("tile") // 2
    rows = 2 * directions
    extra = -(-directions // 16) * 8
    place = [
        jnp.full((tiles, 1), lax.axis_index(axis), jnp.int32) for axis in ("tile", "dir")
    ]
    meta = jnp.concatenate([*place, tile_map, flags], axis=1)

    def memory(*shape, kind=jnp.float32):
        return pltpu.VMEM(shape, kind)

    (packed,) = call(
        pack_kernel,
        [],
        [],
        [jones],
        [],
        [
            memory(*jones.shape),
            memory(rows, LANES),
            pltpu.SemaphoreType.DMA,
            pltpu.SemaphoreType.DMA((chips,)),
        ],
        [(chips, rows, LANES)],
    )
    near = trade(packed)
    narrow = (tiles, directions, samples // 2, 16, BASELINES)
    moments, narrow = call(
        moment_kernel,
        [],
        [],
        [flags, coherency],
        [jax.ShapeDtypeStruct(narrow, coherency.dtype)],
        [
            pltpu.SMEM(flags.shape, flags.dtype),
            memory(*coherency.shape, kind=coherency.dtype),
            memory(tiles, 4, 4 * rows, BASELINES),
            pltpu.SemaphoreType.DMA((tiles, PIECES)),
            pltpu.SemaphoreType.DMA,
            pltpu.SemaphoreType.DMA((tiles, PIECES)),
        ],
        [(tiles, 4, 4 * rows, BASELINES)],
        cost=pl.CostEstimate(
            flops=10 * coherency.size, bytes_accessed=4 * coherency.size, transcendentals=0
        ),
    )
    far = swap_with(near, "tile", 1)

    expanded = (tiles, 2, 4 * rows, LANES)
    of_tile = [(samples, 8, BASELINES), (directions, samples // 2, 2, 8, BASELINES)]
    narrow = pltpu.with_memory_space_constraint(narrow, pltpu.VMEM)
    weight = memory(directions, 12, 8, BASELINES)
    model, row_jones, col_jones, paired = call(
        first_model_kernel,
        [],
        [meta, near, far, narrow],
        [],
        [
            of_tile[0],
            expanded,
            expanded,
            of_tile[1],
        ],
        [weight],
    )
    first = [model, swap_with(model, "dir", 1), row_jones, col_jones, paired]
    model, paired = call(
        functools.partial(next_model_kernel, 1),
        [],
        [narrow, row_jones, col_jones],
        [],
        of_tile,
        [weight],
    )
    last = [model, swap_with(model, "dir", 1), row_jones, col_jones, paired]

    residual_shape = (tiles, samples, 8, LANES)
    terms = (2, 4 * rows, BASELINES)
    scratch = [
        memory(samples, 8, LANES),
        memory(samples // 2, 12, 8, BASELINES),
        pltpu.SemaphoreType.DMA,
    ]
    curvature_terms, masks = call(
        curvature_kernel,
        [],
        [meta, near, far, moments],
        [],
        [(2, tiles, 2 * directions, BASELINES), (tiles, 1 + flags.shape[1], 8, BASELINES)],
        [memory(tiles, 2, 2, 4 * directions, LANES)],
        cost=pl.CostEstimate(
            flops=coherency.size, bytes_accessed=coherency.size, transcendentals=0
        ),
    )
    residual, first_terms = call(
        first_gradient_kernel,
        [],
        [meta, masks, observed, *first],
        [],
        [terms],
        scratch,
        [residual_shape],
    )
    slots = (chips, rows + extra, LANES)
    residual, near, far = call(
        functools.partial(last_gradient_kernel, tiles),
        [],
        [meta, first_terms, curvature_terms, masks, observed, *last],
        [residual],
        [slots, slots],
        [
            memory(*terms),
            *scratch,
            pltpu.SMEM(meta.shape, meta.dtype),
            pltpu.SemaphoreType.DMA,
        ],
        [residual_shape],
        {10: 0},
    )
    parts = trade(near + swap_with(far, "tile", 1))
    directions, _, owned = jones.shape
    in_vmem = pl.BlockSpec(memory_space=pltpu.VMEM)
    gradient, curvature = pl.pallas_call(
        functools.partial(finish_kernel, 1.0 / (samples * SB)),
        in_specs=[in_vmem],
        out_specs=[in_vmem] * 2,
        out_shape=[
            jax.ShapeDtypeStruct(jones.shape, jnp.float32),
            jax.ShapeDtypeStruct((directions, 2, owned), jnp.float32),
        ],
        compiler_params=pltpu.CompilerParams(vmem_limit_bytes=32 * 1024 * 1024),
    )(parts)
    return residual, gradient, curvature


def body(coherency, observed, flags, tile_map, jones):
    jones_all = lax.all_gather(jones, "tile", axis=2, tiled=True)
    how_many = coherency.shape[0]
    predictions = []
    products_list = []
    weight_list = []
    for number in range(how_many):
        predicted, products = tile_terms(
            coherency[number].astype(jnp.float32), jones_all, tile_map[number]
        )
        predictions.append(predicted)
        products_list.append(products)
        weight_list.append(weights(flags[number], tile_map[number]))
    partial_value = jnp.stack(predictions)
    weight = jnp.stack(weight_list)
    columns = observed.shape[3]
    portion = columns // lax.axis_size("dir")
    offset = lax.axis_index("dir") * portion
    summed = lax.psum(partial_value, "dir")
    residual = weight * (observed.astype(jnp.float32) - summed)
    residual_mine = lax.dynamic_slice_in_dim(residual, offset, portion, 3)
    grad_total = jnp.zeros((jones_all.shape[0], 8, jones_all.shape[2]), jnp.float32)
    curv_total = jnp.zeros((jones_all.shape[0], 2, jones_all.shape[2]), jnp.float32)
    for number in range(how_many):
        grad_row, grad_col, curv_row, curv_col = station_terms(
            residual[number], weight[number], products_list[number]
        )
        block_pair = tile_map[number]
        grad_total = add_block(
            add_block(grad_total, grad_row, block_pair[0]), grad_col, block_pair[1]
        )
        curv_total = add_block(
            add_block(curv_total, curv_row, block_pair[0]), curv_col, block_pair[1]
        )
    grad_owned, curv_owned = (
        lax.psum_scatter(grad_total, "tile", scatter_dimension=2, tiled=True),
        lax.psum_scatter(curv_total, "tile", scatter_dimension=2, tiled=True),
    )
    normalizer = 1.0 / (observed.shape[1] * SB)
    return (residual_mine, grad_owned * normalizer, curv_owned * normalizer)


def solution(mesh):
    specs = dict(
        mesh=mesh,
        in_specs=(
            P("tile", "dir", None, None, None),
            P("tile", None, None, None),
            P("tile", None),
            P("tile", None),
            P("dir", None, "tile"),
        ),
        out_specs=(P("tile", None, None, "dir"), P("dir", None, "tile"), P("dir", None, "tile")),
        check_vma=False,
    )

    def run(coherency, observed, flags, tile_map, jones):
        owned = jones.shape[2] // mesh.shape["tile"]
        directions = jones.shape[0] // mesh.shape["dir"]
        fits = owned == 2 * SB and directions % 12 == 0
        paired = mesh.shape["dir"] == 2 and mesh.shape["tile"] == 16
        paired = paired and coherency.shape[0] == 2 * mesh.shape["tile"]
        chosen = body_kernels if fits and paired else body
        return jax.shard_map(chosen, **specs)(coherency, observed, flags, tile_map, jones)

    return run
```

profile of v0, /device:TPU:0, one launch (start us, length us, event | category | flops | bytes accessed | tf_op | source)
XLA Modules:
  0.0 45.9 jit_solution(13364671518737351109)
XLA Ops:
  0.6 0.0 copy-start.2
  0.6 0.0 copy-start.3
  0.7 1.8 %shard_map.76 = f32[8,48,128]{2,1,0:T(8,128)} custom-call(f32[24,8,32]{2,1,0:T(8,128)} %jones_in_hbm.1), custom_call_target="tpu_custom_call" | custom-call | tf_op jit(solution)/shard_map/pallas_call | solution.py:563
  2.4 7.3 %all-to-all-start = ((f32[8,48,128]{2,1,0:T(8,128)}), f32[8,48,128]{2,1,0:T(8,128)S(1)}, u32[]{:S(2)}, u32[]{:S(2)}) async-start(f32[8,48,128]{2,1,0:T(8,128)} %shard_map.76), calls=%async_computation | async-start | bytes 393216 | tf_op jit(solution)/shard_map/all_to_all | solution.py:586
  9.7 4.6 %shard_map.77 = (f32[2,4,192,256]{3,2,1,0:T(8,128)}, bf16[2,24,6,16,256]{4,3,2,1,0:T(8,128)(2,1)S(1)}) custom-call(s32[2,3]{1,0:T(2,128)} %flags_in_hbm.1, bf16[2,24,12,8,256]{4,3,2,1,0:T(8,128)(2,1)} %source.1), custom_call_target="tpu_custom_call" | custom-call | flops 11796480 | bytes 4718592 | tf_op jit(solution)/shard_map/pallas_call | solution.py:563
  14.3 0.1 pad_add_fusion.1
  14.4 3.3 %all-to-all-done.near = f32[8,48,128]{2,1,0:T(8,128)S(1)} async-done(((f32[8,48,128]{2,1,0:T(8,128)}), f32[8,48,128]{2,1,0:T(8,128)S(1)}, u32[]{:S(2)}, u32[]{:S(2)}) %all-to-all-start) | async-done | bytes 196640 | tf_op jit(solution)/shard_map/all_to_all | solution.py:586
  17.7 0.0 collective-permute-start
  17.7 0.0 copy-done.2
  17.7 0.0 copy-done.3
  17.7 0.1 pad_add_fusion.meta.meta_in_vmem
  17.7 1.4 %collective-permute-done.far = f32[8,48,128]{2,1,0:T(8,128)S(1)} collective-permute-done((f32[8,48,128]{2,1,0:T(8,128)S(1)}, f32[8,48,128]{2,1,0:T(8,128)S(1)}, u32[]{:S(2)}, u32[]{:S(2)}) %collective-permute-start) | collective-permute-done | bytes 196640 | tf_op jit(solution)/shard_map/ppermute | solution.py:580
  19.1 0.0 copy-start
  19.1 2.1 %shard_map.79 = (f32[12,8,256]{2,1,0:T(8,128)S(1)}, f32[2,2,192,128]{3,2,1,0:T(8,128)S(1)}, f32[2,2,192,128]{3,2,1,0:T(8,128)S(1)}, f32[24,6,2,8,256]{4,3,2,1,0:T(8,128)S(1)}) custom-call(s32[2,7]{1,0:T(2,128)S(1)} %pad_add_fusion.meta.meta_in_vmem, f32[8,48,128]{2,1,0:T(8,128)S(1)} %all-to-all-done.near, f32[8,48,128]{2,1,0:T(8,128)S(1)} %collective-permute-done.far, ...), custom_call_target="tpu_custom_call" | custom-call | tf_op jit(solution)/shard_map/pallas_call | solution.py:563
  21.2 1.6 %collective-permute-start.1 = (f32[12,8,256]{2,1,0:T(8,128)S(1)}, f32[12,8,256]{2,1,0:T(8,128)S(1)}, u32[]{:S(2)}, u32[]{:S(2)}) collective-permute-start(f32[12,8,256]{2,1,0:T(8,128)S(1)} %get-tuple-element.23.mine), channel_id=1, source_target_pairs={{0,1},{1,0},{2,3},{3,2},{4,5},{5,4},{6,7},{7,6},{8,9},{9,8},{10,11... | collective-permute-start | bytes 294920 | tf_op jit(solution)/shard_map/ppermute | solution.py:580
  22.8 0.0 copy-start.1
  22.8 1.6 %shard_map.81 = (f32[12,8,256]{2,1,0:T(8,128)S(1)}, f32[24,6,2,8,256]{4,3,2,1,0:T(8,128)S(1)}) custom-call(bf16[2,24,6,16,256]{4,3,2,1,0:T(8,128)(2,1)S(1)} %get-tuple-element.22.narrow, f32[2,2,192,128]{3,2,1,0:T(8,128)S(1)} %get-tuple-element.24.row_jones, f32[2,2,192,128]{3,2,1,0:T(8,128)S(1)} %get-tuple-element.25.col_jones), custom_call_target="tpu_custom_call" | custom-call | tf_op jit(solution)/shard_map/pallas_call | solution.py:563
  24.4 0.6 %collective-permute-start.2 = (f32[12,8,256]{2,1,0:T(8,128)S(1)}, f32[12,8,256]{2,1,0:T(8,128)S(1)}, u32[]{:S(2)}, u32[]{:S(2)}) collective-permute-start(f32[12,8,256]{2,1,0:T(8,128)S(1)} %get-tuple-element.29.mine), channel_id=1, source_target_pairs={{0,1},{1,0},{2,3},{3,2},{4,5},{5,4},{6,7},{7,6},{8,9},{9,8},{10,11... | collective-permute-start | bytes 294920 | tf_op jit(solution)/shard_map/ppermute | solution.py:580
  25.0 0.0 copy-done
  25.0 1.2 %shard_map.78 = (f32[2,2,48,256]{3,2,1,0:T(8,128)S(1)}, f32[2,4,8,256]{3,2,1,0:T(8,128)S(1)}) custom-call(s32[2,7]{1,0:T(2,128)S(1)} %pad_add_fusion.meta.meta_in_vmem, f32[8,48,128]{2,1,0:T(8,128)S(1)} %all-to-all-done.near, f32[8,48,128]{2,1,0:T(8,128)S(1)} %collective-permute-done.far, f32[2,4,192,256]{3,2,1,0:T(8,128)S(1)} %copy-done), custom_call_target="tpu_custom_call" | custom-call | flops 1179648 | bytes 1179648 | tf_op jit(solution)/shard_map/pallas_call | solution.py:563
  26.2 0.0 collective-permute-done.1.other
  26.2 0.0 copy-done.1
  26.2 1.8 %shard_map.80 = (f32[2,12,8,128]{3,2,1,0:T(8,128)}, f32[2,192,256]{2,1,0:T(8,128)S(1)}) custom-call(s32[2,7]{1,0:T(2,128)S(1)} %pad_add_fusion.meta.meta_in_vmem, f32[2,4,8,256]{3,2,1,0:T(8,128)S(1)} %get-tuple-element.21.masks, bf16[2,12,8,256]{3,2,1,0:T(8,128)(2,1)S(1)} %copy-done.1, f32[12,8,256]{2,1,0:T(8,128)S(1)} %get-tuple-element.23.mine, ...), custom_call_target="tpu_custom_call" | custom-call | tf_op jit(solution)/shard_map/pallas_call | solution.py:563
  28.0 1.1 %collective-permute-done.2.other = f32[12,8,256]{2,1,0:T(8,128)S(1)} collective-permute-done((f32[12,8,256]{2,1,0:T(8,128)S(1)}, f32[12,8,256]{2,1,0:T(8,128)S(1)}, u32[]{:S(2)}, u32[]{:S(2)}) %collective-permute-start.2) | collective-permute-done | bytes 98336 | tf_op jit(solution)/shard_map/ppermute | solution.py:580
  29.1 2.3 %shard_map.82 = (f32[2,12,8,128]{3,2,1,0:T(8,128)}, f32[8,64,128]{2,1,0:T(8,128)S(1)}, f32[8,64,128]{2,1,0:T(8,128)S(1)}) custom-call(s32[2,7]{1,0:T(2,128)S(1)} %pad_add_fusion.meta.meta_in_vmem, f32[2,192,256]{2,1,0:T(8,128)S(1)} %get-tuple-element.27.first_terms, ...), custom_call_target="tpu_custom_call", output_to_operand_aliasing={{0}: (10, {})} | custom-call | tf_op jit(solution)/shard_map/pallas_call | solution.py:563
  31.4 0.1 collective-permute-start.3
  31.5 1.5 %collective-permute-done.3 = f32[8,64,128]{2,1,0:T(8,128)S(1)} collective-permute-done((f32[8,64,128]{2,1,0:T(8,128)S(1)}, f32[8,64,128]{2,1,0:T(8,128)S(1)}, u32[]{:S(2)}, u32[]{:S(2)}) %collective-permute-start.3) | collective-permute-done | bytes 262176 | tf_op jit(solution)/shard_map/ppermute | solution.py:580
  33.1 12.2 %all_to_all.10.parts = f32[8,64,128]{2,1,0:T(8,128)S(1)} all-to-all(f32[8,64,128]{2,1,0:T(8,128)S(1)} %add.3), channel_id=1, replica_groups={{0,4,8,12,16,20,24,28},{2,6,10,14,18,22,26,30},{1,5,9,13,17,21,25,29},{..., dimensions={0} | all-to-all | bytes 524288 | tf_op jit(solution)/shard_map/all_to_all | solution.py:586
  45.2 0.7 %shard_map.83 = (f32[24,8,32]{2,1,0:T(8,128)}, f32[24,2,32]{2,1,0:T(2,128)}) custom-call(f32[8,64,128]{2,1,0:T(8,128)S(1)} %all_to_all.10.parts), custom_call_target="tpu_custom_call" | custom-call | tf_op jit(solution)/shard_map/pallas_call | solution.py:713
  (1 shorter events, 0.0 us)
Async XLA Ops:
  0.6 17.0 %copy-start.2 = (s32[2,3]{1,0:T(2,128)S(1)}, s32[2,3]{1,0:T(2,128)}, u32[]{:S(2)}) copy-start(s32[2,3]{1,0:T(2,128)} %flags_in_hbm.1) | copy-start | bytes 76
  0.6 17.0 %copy-start.3 = (s32[2,2]{1,0:T(2,128)S(1)}, s32[2,2]{1,0:T(2,128)}, u32[]{:S(2)}) copy-start(s32[2,2]{1,0:T(2,128)} %param.8) | copy-start | bytes 52
  2.4 15.2 %all-to-all-start = ((f32[8,48,128]{2,1,0:T(8,128)}), f32[8,48,128]{2,1,0:T(8,128)S(1)}, u32[]{:S(2)}, u32[]{:S(2)}) async-start(f32[8,48,128]{2,1,0:T(8,128)} %shard_map.76), calls=%async_computation | async-start | bytes 393216 | tf_op jit(solution)/shard_map/all_to_all | solution.py:586
  17.7 1.4 %collective-permute-start = (f32[8,48,128]{2,1,0:T(8,128)S(1)}, f32[8,48,128]{2,1,0:T(8,128)S(1)}, u32[]{:S(2)}, u32[]{:S(2)}) collective-permute-start(f32[8,48,128]{2,1,0:T(8,128)S(1)} %all-to-all-done.near), channel_id=1, source_target_pairs={{0,2},{2,0},{4,6},{6,4},{8,10},{10,8},{12,14},{14,12},{16,18},{18,... | collective-permute-start | bytes 589832 | tf_op jit(solution)/shard_map/ppermute | solution.py:580
  19.1 5.9 %copy-start = (f32[2,4,192,256]{3,2,1,0:T(8,128)S(1)}, f32[2,4,192,256]{3,2,1,0:T(8,128)}, u32[]{:S(2)}) copy-start(f32[2,4,192,256]{3,2,1,0:T(8,128)} %get-tuple-element.20.moments) | copy-start | bytes 4718596
  21.2 5.0 %collective-permute-start.1 = (f32[12,8,256]{2,1,0:T(8,128)S(1)}, f32[12,8,256]{2,1,0:T(8,128)S(1)}, u32[]{:S(2)}, u32[]{:S(2)}) collective-permute-start(f32[12,8,256]{2,1,0:T(8,128)S(1)} %get-tuple-element.23.mine), channel_id=1, source_target_pairs={{0,1},{1,0},{2,3},{3,2},{4,5},{5,4},{6,7},{7,6},{8,9},{9,8},{10,11... | collective-permute-start | bytes 294920 | tf_op jit(solution)/shard_map/ppermute | solution.py:580
  22.8 3.4 %copy-start.1 = (bf16[2,12,8,256]{3,2,1,0:T(8,128)(2,1)S(1)}, bf16[2,12,8,256]{3,2,1,0:T(8,128)(2,1)}, u32[]{:S(2)}) copy-start(bf16[2,12,8,256]{3,2,1,0:T(8,128)(2,1)} %observed.3) | copy-start | bytes 294916
  24.4 4.7 %collective-permute-start.2 = (f32[12,8,256]{2,1,0:T(8,128)S(1)}, f32[12,8,256]{2,1,0:T(8,128)S(1)}, u32[]{:S(2)}, u32[]{:S(2)}) collective-permute-start(f32[12,8,256]{2,1,0:T(8,128)S(1)} %get-tuple-element.29.mine), channel_id=1, source_target_pairs={{0,1},{1,0},{2,3},{3,2},{4,5},{5,4},{6,7},{7,6},{8,9},{9,8},{10,11... | collective-permute-start | bytes 294920 | tf_op jit(solution)/shard_map/ppermute | solution.py:580
  31.4 1.6 %collective-permute-start.3 = (f32[8,64,128]{2,1,0:T(8,128)S(1)}, f32[8,64,128]{2,1,0:T(8,128)S(1)}, u32[]{:S(2)}, u32[]{:S(2)}) collective-permute-start(f32[8,64,128]{2,1,0:T(8,128)S(1)} %get-tuple-element.34), channel_id=1, source_target_pairs={{0,2},{2,0},{4,6},{6,4},{8,10},{10,8},{12,14},{14,12},{16,18},{18,... | collective-permute-start | bytes 786440 | tf_op jit(solution)/shard_map/ppermute | solution.py:580
where the time goes:
time: 46.2 us; the launch traced here: 45.9 us
  Pallas kernels  16.1 us (35%)
  blocking collectives  12.2 us (26%)
  starting transfers between devices  9.52 us (21%)
  waiting for transfers between devices  7.24 us (16%)
  between operations  0.73 us (2%)
    pallas_call x7, Pallas kernels, call(): pl.pallas_call(kernel, in_specs=[place(space) for space in spaces], out_s...  15.4 us
    all_to_all x1, blocking collectives, trade(): lax.all_to_all(slots, 'tile', 0, 0, axis_index_groups=groups, tiled=True)  12.2 us
    all_to_all x1, starting transfers between devices, trade(): lax.all_to_all(slots, 'tile', 0, 0, axis_index_groups=groups, tiled=True)  7.29 us
    ppermute x4, waiting for transfers between devices, swap_with(): lax.ppermute(value, axis, [(place, place ^ mask) for place in range(size)])  3.97 us
    all_to_all x1, waiting for transfers between devices, trade(): lax.all_to_all(slots, 'tile', 0, 0, axis_index_groups=groups, tiled=True)  3.27 us
    ppermute x4, starting transfers between devices, swap_with(): lax.ppermute(value, axis, [(place, place ^ mask) for place in range(size)])  2.23 us
  transfers between devices with their start and end apart: 5, of which 4 were waited for; matrix products, arithmetic and copies ran while one was open for 0% of the time, Pallas kernels for 20%

commit v1 on v0

--- a/solution.py
+++ b/solution.py
@@ -117,6 +117,12 @@
     return jnp.where(low, first, turn(second, 4)), jnp.where(low, turn(first, 4), second)
 
 
+def add_all(sums, values):
+    if sums is None:
+        return values
+    return [v if total is None else total + v for total, v in zip(sums, values)]
+
+
 def halves(value):
     high = value.astype(jnp.bfloat16)
     return high, (value - high.astype(jnp.float32)).astype(jnp.bfloat16)
@@ -155,9 +161,8 @@
     return total[:count] + total[count:]
 
 
-def to_lanes(parts, half):
-    moved = [pltpu.roll(part, 2 * SB * g + SB * half, 1) for g, part in enumerate(parts)]
-    return sum(moved[1:], moved[0])
+def to_lanes(parts):
+    return sum((pltpu.roll(part, 2 * SB * g, 1) for g, part in enumerate(parts) if g), parts[0])
 
 
 def arranged(ref, tile, half, k, mask):
@@ -178,22 +183,17 @@
     return jnp.where((baseline // SB < baseline % SB) | above, 1.0, 0.0).astype(jnp.float32)
 
 
-def pack_kernel(jones_in_hbm, slots, jones, packed, in_semaphore, semaphores):
-    copy = pltpu.make_async_copy(jones_in_hbm, jones, in_semaphore)
+def pack_kernel(jones_in_hbm, packed, jones, semaphore):
+    copy = pltpu.make_async_copy(jones_in_hbm, jones, semaphore)
     copy.start()
     copy.wait()
     each = jones.shape[0] // 4
-    rows = packed.shape[0]
-    packed[...] = jnp.concatenate(
+    rows = packed.shape[1]
+    made = jnp.concatenate(
         [jones[g * each : (g + 1) * each].reshape(rows, 2 * SB) for g in range(4)], axis=1
     )
-    copies = [
-        pltpu.make_async_copy(packed, slots.at[n], semaphores.at[n]) for n in range(slots.shape[0])
-    ]
-    for copy in copies:
-        copy.start()
-    for copy in copies:
-        copy.wait()
+    for copy in range(packed.shape[0]):
+        packed[copy] = made
 
 
 def entry(meta, row, column, shape=(8, LANES)):
@@ -214,6 +214,8 @@
 
 
 PIECES = 6
+SPARE_ROWS = 8
+BLOCK_NUMBERS = 64
 
 
 def block_of(meta, tile, side):
@@ -307,7 +309,9 @@
     for side, jones in enumerate((row_jones, col_jones)):
         found = [station_block(meta, near, far, tile, side) for tile in range(tiles)]
         for tile, made in enumerate(expand(found, side == 0)):
-            jones[tile, 0], jones[tile, 1] = made[:, :LANES], made[:, LANES:]
+            for half in range(2):
+                lanes = slice(half * LANES, (half + 1) * LANES)
+                jones[tile, half, : made.shape[0]] = made[:, lanes]
     models(0, narrow, row_jones, col_jones, model, paired, weight)
 
 
@@ -339,7 +343,7 @@
         first = step // 2 * CHUNK
         zero = jnp.zeros((8, LANES), jnp.float32)
         low = component(zero) < 4
-        sums = [[zero] * CHUNK for n in range(12)]
+        sums = [None] * 12
         for k in range(directions):
             parts = []
             for i in range(CHUNK):
@@ -350,7 +354,7 @@
                 parts.append((real + imag, real, imag))
             for n in range(12):
                 w = weight[k, n, :, lanes]
-                sums[n] = [sums[n][i] + w * parts[i][n % 3] for i in range(CHUNK)]
+                sums[n] = add_all(sums[n], [w * parts[i][n % 3] for i in range(CHUNK)])
         for i in range(CHUNK):
             one, two, three = ([sums[3 * x + m][i] for x in range(4)] for m in range(3))
             real = fold([one[x] - three[x] for x in range(4)])
@@ -376,7 +380,8 @@
         made = expand([station_products(packed) for packed in found], side == 0)
         for tile in range(tiles):
             for half in range(2):
-                products[tile, side, half] = made[tile][:, half * LANES : (half + 1) * LANES]
+                lanes = slice(half * LANES, (half + 1) * LANES)
+                products[tile, side, half, : made[tile].shape[0]] = made[tile][:, lanes]
 
     def combine(step, _):
         tile, group = step // (directions // 4), step % (directions // 4)
@@ -415,11 +420,10 @@
     lax.fori_loop(0, tiles * directions // 4, combine, 0)
 
 
-def add_to_owner(meta, near, far, block, part):
+def add_to_owner(meta, near, block, part):
     owner = block // 2
     own_core = jnp.where(owner % 2 == meta[0, 0] % 2, 1.0, 0.0)
-    near[owner // 2] = near[owner // 2] + own_core * part
-    far[owner // 2] = far[owner // 2] + (1.0 - own_core) * part
+    near[owner // 2] = near[owner // 2] + own_core * pltpu.roll(part, SB * (block % 2), 1)
 
 
 def add_gradient_terms(
@@ -451,7 +455,7 @@
         half, lanes = step % 2, half_lanes(step % 2)
         first = step // 2 * CHUNK
         zero = jnp.zeros((8, LANES), jnp.float32)
-        sums = [[zero] * CHUNK for n in range(12)]
+        sums = [None] * 12
         for p in range(pairs):
             parts = []
             for i in range(CHUNK):
@@ -460,7 +464,7 @@
                 parts.append((real + imag, real, imag))
             for n in range(12):
                 r = turned[p, n, :, lanes]
-                sums[n] = [sums[n][i] + r * parts[i][n % 3] for i in range(CHUNK)]
+                sums[n] = add_all(sums[n], [r * parts[i][n % 3] for i in range(CHUNK)])
         bits = component(zero)
         real = bits < 4
         equal = (bits >> 1) & 1 == bits & 1
@@ -468,8 +472,8 @@
             k = first + i
             p_re, p_im = arranged(row_jones, tile, half, k, 2)
             q_re, q_im = arranged(col_jones, tile, half, k, 1)
-            row_sum = [zero, zero]
-            col_sum = [zero, zero]
+            row_sum = [None, None]
+            col_sum = [None, None]
             for x in range(4):
                 a, b = x // 2, x % 2
                 y_re = sums[3 * x][i] - sums[3 * x + 2][i]
@@ -477,8 +481,8 @@
                 y_re = y_re + turn(y_re, 4)
                 y_im = y_im + turn(y_im, 4)
                 one, two = jnp.where(real, y_re, y_im), jnp.where(real, -y_im, y_re)
-                row_sum[a] = row_sum[a] + (q_re[b] * one + q_im[b] * two)
-                col_sum[b] = col_sum[b] + (p_re[a] * one - p_im[a] * two)
+                (row_sum[a],) = add_all(row_sum[a : a + 1], [q_re[b] * one + q_im[b] * two])
+                (col_sum[b],) = add_all(col_sum[b : b + 1], [p_re[a] * one - p_im[a] * two])
             rows = pl.ds(pl.multiple_of(8 * k, 8), 8)
             g, h = row_sum
             g = jnp.where(equal, g, h) + flip(jnp.where(equal, h, g), 1)
@@ -506,7 +510,7 @@
 def last_gradient_kernel(
     tiles, meta_in_vmem, first_terms, curvature_terms,
     masks, observed, mine, other, row_jones, col_jones, paired,
-    residual_before, residual_out, near, far, terms, residual, turned, semaphore,
+    residual_before, residual_out, near, compact, terms, residual, turned, semaphore,
     meta, meta_semaphore,
 ):
     del residual_before
@@ -517,17 +521,16 @@
         residual_out, terms, residual, turned, semaphore,
     )
     near[...] = jnp.zeros_like(near)
-    far[...] = jnp.zeros_like(far)
     meta_copy.wait()
     directions = paired.shape[0]
     rows, few = 8 * directions, 2 * directions
-    for side, blocks in enumerate(sides(meta, tiles)):
+    both_sides = sides(meta, tiles)
+    for side, blocks in enumerate(both_sides):
         stack = [first_terms[side], terms[side]]
         stack.extend(curvature_terms[side, tile] for tile in range(tiles))
         sums = station_sums(jnp.concatenate(stack, axis=0), side == 0)
         for tile, block in enumerate(blocks):
-            half = block % 2
-            part = to_lanes(jnp.split(sums[tile * rows : (tile + 1) * rows], 4, axis=0), half)
+            part = to_lanes(jnp.split(sums[tile * rows : (tile + 1) * rows], 4, axis=0))
             part = part.reshape(-1, 8, LANES)
             if side == 0:
                 part = transpose_matrix(part)
@@ -536,9 +539,40 @@
             start = tiles * rows + tile * few
             groups = jnp.split(sums[start : start + few], directions // 4, axis=0)
             chosen = [groups[n : n + 4] for n in range(0, len(groups), 4)]
-            made = [part.reshape(-1, LANES), *(to_lanes(parts, half) for parts in chosen)]
-            add_to_owner(meta, near, far, block, jnp.concatenate(made, axis=0))
+            made = [part.reshape(-1, LANES), *(to_lanes(parts) for parts in chosen)]
+            part = jnp.concatenate(made, axis=0)
+            add_to_owner(meta, near, block, part)
+            compact[tile] = part if side == 0 else compact[tile] + pltpu.roll(part, SB, 1)
+    lane = lax.broadcasted_iota(jnp.int32, (8, LANES), 1)
+    for tile in range(tiles):
+        numbers = [blocks[tile].astype(jnp.float32) for blocks in both_sides]
+        number = jnp.where(lane < BLOCK_NUMBERS + 2 * SB, *numbers)
+        compact[tile, -8:] = jnp.where(lane < BLOCK_NUMBERS, compact[tile, -8:], number)
     sent.wait()
+
+
+def merge_kernel(meta, near, compact, total):
+    slots, rows = near.shape[:2]
+    lane = lax.broadcasted_iota(jnp.int32, (8, LANES), 1)
+    found = []
+    for tile in range(compact.shape[0]):
+        value = compact[tile]
+        for side in range(2):
+            start = BLOCK_NUMBERS + 2 * SB * side
+            number = jnp.broadcast_to(value[-8:, start : start + 1], (8, LANES))
+            block = number.astype(jnp.int32)
+            owner = block >> 1
+            slot = jnp.where((owner ^ entry(meta, 0, 0)) & 1 == 0, owner >> 1, -1)
+            shifted = pltpu.roll(value, SB if side == 0 else LANES - SB, 1)
+            stays = block & 1 == side
+            part = jnp.where(stays, value.reshape(-1, 8, LANES), shifted.reshape(-1, 8, LANES))
+            part = jnp.where((lane // SB) & 1 == block & 1, part, 0.0)
+            found.append((slot, part))
+    for n in range(slots):
+        out = near[n].reshape(-1, 8, LANES)
+        for slot, part in found:
+            out = out + jnp.where(slot == n, part, 0.0)
+        total[n] = out.reshape(rows, LANES)
 
 
 def finish_kernel(normalizer, parts, gradient, curvature):
@@ -604,14 +638,8 @@
         [],
         [],
         [jones],
-        [],
-        [
-            memory(*jones.shape),
-            memory(rows, LANES),
-            pltpu.SemaphoreType.DMA,
-            pltpu.SemaphoreType.DMA((chips,)),
-        ],
         [(chips, rows, LANES)],
+        [memory(*jones.shape), pltpu.SemaphoreType.DMA],
     )
     near = trade(packed)
     narrow = (tiles, directions, samples // 2, 16, BASELINES)
@@ -636,7 +664,7 @@
     )
     far = swap_with(near, "tile", 1)
 
-    expanded = (tiles, 2, 4 * rows, LANES)
+    expanded = (tiles, 2, 4 * rows + SPARE_ROWS, LANES)
     of_tile = [(samples, 8, BASELINES), (directions, samples // 2, 2, 8, BASELINES)]
     narrow = pltpu.with_memory_space_constraint(narrow, pltpu.VMEM)
     weight = memory(directions, 12, 8, BASELINES)
@@ -677,7 +705,7 @@
         [meta, near, far, moments],
         [],
         [(2, tiles, 2 * directions, BASELINES), (tiles, 1 + flags.shape[1], 8, BASELINES)],
-        [memory(tiles, 2, 2, 4 * directions, LANES)],
+        [memory(tiles, 2, 2, 4 * directions + SPARE_ROWS, LANES)],
         cost=pl.CostEstimate(
             flops=coherency.size, bytes_accessed=coherency.size, transcendentals=0
         ),
@@ -692,12 +720,12 @@
         [residual_shape],
     )
     slots = (chips, rows + extra, LANES)
-    residual, near, far = call(
+    residual, near, compact = call(
         functools.partial(last_gradient_kernel, tiles),
         [],
         [meta, first_terms, curvature_terms, masks, observed, *last],
         [residual],
-        [slots, slots],
+        [slots, (tiles,) + slots[1:]],
         [
             memory(*terms),
             *scratch,
@@ -707,7 +735,9 @@
         [residual_shape],
         {10: 0},
     )
-    parts = trade(near + swap_with(far, "tile", 1))
+    theirs = swap_with(compact, "tile", 1)
+    (total,) = call(merge_kernel, [], [meta, near, theirs], [], [slots])
+    parts = trade(total)
     directions, _, owned = jones.shape
     in_vmem = pl.BlockSpec(memory_space=pltpu.VMEM)
     gradient, curvature = pl.pallas_call(
@@ -782,7 +812,7 @@
     def run(coherency, observed, flags, tile_map, jones):
         owned = jones.shape[2] // mesh.shape["tile"]
         directions = jones.shape[0] // mesh.shape["dir"]
-        fits = owned == 2 * SB and directions % 12 == 0
+        fits = owned == 2 * SB and directions == 24
         paired = mesh.shape["dir"] == 2 and mesh.shape["tile"] == 16
         paired = paired and coherency.shape[0] == 2 * mesh.shape["tile"]
         chosen = body_kernels if fits and paired else body

time: 46.2 us -> 46.1 us (level)
    pallas_call x7 -> x8, Pallas kernels: 15.4 us -> 15.5 us  [call(): pl.pallas_call(kernel, in_specs=[place(space) for space in spaces], out_s...]
where the time goes in v1:
time: 46.1 us; the launch traced here: 45.8 us
  Pallas kernels  16.2 us (35%)
  blocking collectives  12.2 us (26%)
  starting transfers between devices  9.52 us (21%)
  waiting for transfers between devices  6.96 us (15%)
  between operations  0.74 us (2%)
    pallas_call x8, Pallas kernels, call(): pl.pallas_call(kernel, in_specs=[place(space) for space in spaces], out_s...  15.5 us
    all_to_all x1, blocking collectives, trade(): lax.all_to_all(slots, 'tile', 0, 0, axis_index_groups=groups, tiled=True)  12.2 us
    all_to_all x1, starting transfers between devices, trade(): lax.all_to_all(slots, 'tile', 0, 0, axis_index_groups=groups, tiled=True)  7.29 us
    ppermute x4, waiting for transfers between devices, swap_with(): lax.ppermute(value, axis, [(place, place ^ mask) for place in range(size)])  3.69 us
    all_to_all x1, waiting for transfers between devices, trade(): lax.all_to_all(slots, 'tile', 0, 0, axis_index_groups=groups, tiled=True)  3.27 us
    ppermute x4, starting transfers between devices, swap_with(): lax.ppermute(value, axis, [(place, place ^ mask) for place in range(size)])  2.23 us
  transfers between devices with their start and end apart: 5, of which 4 were waited for; matrix products, arithmetic and copies ran while one was open for 0% of the time, Pallas kernels for 20%

profile of v1, /device:TPU:0, one launch (start us, length us, event | category | flops | bytes accessed | tf_op | source)
XLA Modules:
  0.0 45.8 jit_solution(4029994833659470861)
XLA Ops:
  0.6 0.0 copy-start.2
  0.6 0.0 copy-start.3
  0.7 1.7 %shard_map.76 = f32[8,48,128]{2,1,0:T(8,128)} custom-call(f32[24,8,32]{2,1,0:T(8,128)} %jones_in_hbm.1), custom_call_target="tpu_custom_call" | custom-call | tf_op jit(solution)/shard_map/pallas_call | solution.py:597
  2.3 7.3 %all-to-all-start = ((f32[8,48,128]{2,1,0:T(8,128)}), f32[8,48,128]{2,1,0:T(8,128)S(1)}, u32[]{:S(2)}, u32[]{:S(2)}) async-start(f32[8,48,128]{2,1,0:T(8,128)} %shard_map.76), calls=%async_computation | async-start | bytes 393216 | tf_op jit(solution)/shard_map/all_to_all | solution.py:620
  9.6 4.6 %shard_map.77 = (f32[2,4,192,256]{3,2,1,0:T(8,128)}, bf16[2,24,6,16,256]{4,3,2,1,0:T(8,128)(2,1)S(1)}) custom-call(s32[2,3]{1,0:T(2,128)} %flags_in_hbm.1, bf16[2,24,12,8,256]{4,3,2,1,0:T(8,128)(2,1)} %source.1), custom_call_target="tpu_custom_call" | custom-call | flops 11796480 | bytes 4718592 | tf_op jit(solution)/shard_map/pallas_call | solution.py:597
  14.2 0.1 pad_add_fusion.1
  14.3 3.3 %all-to-all-done.near = f32[8,48,128]{2,1,0:T(8,128)S(1)} async-done(((f32[8,48,128]{2,1,0:T(8,128)}), f32[8,48,128]{2,1,0:T(8,128)S(1)}, u32[]{:S(2)}, u32[]{:S(2)}) %all-to-all-start) | async-done | bytes 196640 | tf_op jit(solution)/shard_map/all_to_all | solution.py:620
  17.6 0.0 collective-permute-start
  17.6 0.0 copy-done.2
  17.6 0.0 copy-done.3
  17.6 0.1 pad_add_fusion.meta.meta_in_vmem
  17.7 1.4 %collective-permute-done.far = f32[8,48,128]{2,1,0:T(8,128)S(1)} collective-permute-done((f32[8,48,128]{2,1,0:T(8,128)S(1)}, f32[8,48,128]{2,1,0:T(8,128)S(1)}, u32[]{:S(2)}, u32[]{:S(2)}) %collective-permute-start) | collective-permute-done | bytes 196640 | tf_op jit(solution)/shard_map/ppermute | solution.py:614
  19.0 0.0 copy-start
  19.0 2.1 %shard_map.79 = (f32[12,8,256]{2,1,0:T(8,128)S(1)}, f32[2,2,200,128]{3,2,1,0:T(8,128)S(1)}, f32[2,2,200,128]{3,2,1,0:T(8,128)S(1)}, f32[24,6,2,8,256]{4,3,2,1,0:T(8,128)S(1)}) custom-call(s32[2,7]{1,0:T(2,128)S(1)} %pad_add_fusion.meta.meta_in_vmem, f32[8,48,128]{2,1,0:T(8,128)S(1)} %all-to-all-done.near, f32[8,48,128]{2,1,0:T(8,128)S(1)} %collective-permute-done.far, ...), custom_call_target="tpu_custom_call" | custom-call | tf_op jit(solution)/shard_map/pallas_call | solution.py:597
  21.2 1.6 %collective-permute-start.1 = (f32[12,8,256]{2,1,0:T(8,128)S(1)}, f32[12,8,256]{2,1,0:T(8,128)S(1)}, u32[]{:S(2)}, u32[]{:S(2)}) collective-permute-start(f32[12,8,256]{2,1,0:T(8,128)S(1)} %get-tuple-element.23.mine), channel_id=1, source_target_pairs={{0,1},{1,0},{2,3},{3,2},{4,5},{5,4},{6,7},{7,6},{8,9},{9,8},{10,11... | collective-permute-start | bytes 294920 | tf_op jit(solution)/shard_map/ppermute | solution.py:614
  22.7 0.0 copy-start.1
  22.7 1.6 %shard_map.81 = (f32[12,8,256]{2,1,0:T(8,128)S(1)}, f32[24,6,2,8,256]{4,3,2,1,0:T(8,128)S(1)}) custom-call(bf16[2,24,6,16,256]{4,3,2,1,0:T(8,128)(2,1)S(1)} %get-tuple-element.22.narrow, f32[2,2,200,128]{3,2,1,0:T(8,128)S(1)} %get-tuple-element.24.row_jones, f32[2,2,200,128]{3,2,1,0:T(8,128)S(1)} %get-tuple-element.25.col_jones), custom_call_target="tpu_custom_call" | custom-call | tf_op jit(solution)/shard_map/pallas_call | solution.py:597
  24.3 0.6 %collective-permute-start.2 = (f32[12,8,256]{2,1,0:T(8,128)S(1)}, f32[12,8,256]{2,1,0:T(8,128)S(1)}, u32[]{:S(2)}, u32[]{:S(2)}) collective-permute-start(f32[12,8,256]{2,1,0:T(8,128)S(1)} %get-tuple-element.29.mine), channel_id=1, source_target_pairs={{0,1},{1,0},{2,3},{3,2},{4,5},{5,4},{6,7},{7,6},{8,9},{9,8},{10,11... | collective-permute-start | bytes 294920 | tf_op jit(solution)/shard_map/ppermute | solution.py:614
  24.9 0.0 copy-done
  24.9 1.2 %shard_map.78 = (f32[2,2,48,256]{3,2,1,0:T(8,128)S(1)}, f32[2,4,8,256]{3,2,1,0:T(8,128)S(1)}) custom-call(s32[2,7]{1,0:T(2,128)S(1)} %pad_add_fusion.meta.meta_in_vmem, f32[8,48,128]{2,1,0:T(8,128)S(1)} %all-to-all-done.near, f32[8,48,128]{2,1,0:T(8,128)S(1)} %collective-permute-done.far, f32[2,4,192,256]{3,2,1,0:T(8,128)S(1)} %copy-done), custom_call_target="tpu_custom_call" | custom-call | flops 1179648 | bytes 1179648 | tf_op jit(solution)/shard_map/pallas_call | solution.py:597
  26.1 0.0 collective-permute-done.1.other
  26.1 0.0 copy-done.1
  26.1 1.8 %shard_map.80 = (f32[2,12,8,128]{3,2,1,0:T(8,128)}, f32[2,192,256]{2,1,0:T(8,128)S(1)}) custom-call(s32[2,7]{1,0:T(2,128)S(1)} %pad_add_fusion.meta.meta_in_vmem, f32[2,4,8,256]{3,2,1,0:T(8,128)S(1)} %get-tuple-element.21.masks, bf16[2,12,8,256]{3,2,1,0:T(8,128)(2,1)S(1)} %copy-done.1, f32[12,8,256]{2,1,0:T(8,128)S(1)} %get-tuple-element.23.mine, ...), custom_call_target="tpu_custom_call" | custom-call | tf_op jit(solution)/shard_map/pallas_call | solution.py:597
  27.9 1.1 %collective-permute-done.2.other = f32[12,8,256]{2,1,0:T(8,128)S(1)} collective-permute-done((f32[12,8,256]{2,1,0:T(8,128)S(1)}, f32[12,8,256]{2,1,0:T(8,128)S(1)}, u32[]{:S(2)}, u32[]{:S(2)}) %collective-permute-start.2) | collective-permute-done | bytes 98336 | tf_op jit(solution)/shard_map/ppermute | solution.py:614
  29.0 2.4 %shard_map.82 = (f32[2,12,8,128]{3,2,1,0:T(8,128)}, f32[8,64,128]{2,1,0:T(8,128)S(1)}, f32[2,64,128]{2,1,0:T(8,128)S(1)}) custom-call(s32[2,7]{1,0:T(2,128)S(1)} %pad_add_fusion.meta.meta_in_vmem, f32[2,192,256]{2,1,0:T(8,128)S(1)} %get-tuple-element.27.first_terms, ...), custom_call_target="tpu_custom_call", output_to_operand_aliasing={{0}: (10, {})} | custom-call | tf_op jit(solution)/shard_map/pallas_call | solution.py:597
  31.4 0.1 collective-permute-start.3
  31.5 1.2 %collective-permute-done.3.compact = f32[2,64,128]{2,1,0:T(8,128)S(1)} collective-permute-done((f32[2,64,128]{2,1,0:T(8,128)S(1)}, f32[2,64,128]{2,1,0:T(8,128)S(1)}, u32[]{:S(2)}, u32[]{:S(2)}) %collective-permute-start.3) | collective-permute-done | bytes 65568 | tf_op jit(solution)/shard_map/ppermute | solution.py:614
  32.7 0.2 shard_map.83
  32.9 12.2 %all_to_all.10.parts = f32[8,64,128]{2,1,0:T(8,128)S(1)} all-to-all(f32[8,64,128]{2,1,0:T(8,128)S(1)} %shard_map.83), channel_id=1, replica_groups={{0,4,8,12,16,20,24,28},{2,6,10,14,18,22,26,30},{1,5,9,13,17,21,25,29},{..., dimensions={0} | all-to-all | bytes 524288 | tf_op jit(solution)/shard_map/all_to_all | solution.py:620
  45.1 0.7 %shard_map.84 = (f32[24,8,32]{2,1,0:T(8,128)}, f32[24,2,32]{2,1,0:T(2,128)}) custom-call(f32[8,64,128]{2,1,0:T(8,128)S(1)} %all_to_all.10.parts), custom_call_target="tpu_custom_call" | custom-call | tf_op jit(solution)/shard_map/pallas_call | solution.py:743
Async XLA Ops:
  0.6 17.0 %copy-start.2 = (s32[2,3]{1,0:T(2,128)S(1)}, s32[2,3]{1,0:T(2,128)}, u32[]{:S(2)}) copy-start(s32[2,3]{1,0:T(2,128)} %flags_in_hbm.1) | copy-start | bytes 76
  0.6 17.0 %copy-start.3 = (s32[2,2]{1,0:T(2,128)S(1)}, s32[2,2]{1,0:T(2,128)}, u32[]{:S(2)}) copy-start(s32[2,2]{1,0:T(2,128)} %param.8) | copy-start | bytes 52
  2.3 15.2 %all-to-all-start = ((f32[8,48,128]{2,1,0:T(8,128)}), f32[8,48,128]{2,1,0:T(8,128)S(1)}, u32[]{:S(2)}, u32[]{:S(2)}) async-start(f32[8,48,128]{2,1,0:T(8,128)} %shard_map.76), calls=%async_computation | async-start | bytes 393216 | tf_op jit(solution)/shard_map/all_to_all | solution.py:620
  17.6 1.4 %collective-permute-start = (f32[8,48,128]{2,1,0:T(8,128)S(1)}, f32[8,48,128]{2,1,0:T(8,128)S(1)}, u32[]{:S(2)}, u32[]{:S(2)}) collective-permute-start(f32[8,48,128]{2,1,0:T(8,128)S(1)} %all-to-all-done.near), channel_id=1, source_target_pairs={{0,2},{2,0},{4,6},{6,4},{8,10},{10,8},{12,14},{14,12},{16,18},{18,... | collective-permute-start | bytes 589832 | tf_op jit(solution)/shard_map/ppermute | solution.py:614
  19.0 5.9 %copy-start = (f32[2,4,192,256]{3,2,1,0:T(8,128)S(1)}, f32[2,4,192,256]{3,2,1,0:T(8,128)}, u32[]{:S(2)}) copy-start(f32[2,4,192,256]{3,2,1,0:T(8,128)} %get-tuple-element.20.moments) | copy-start | bytes 4718596
  21.2 5.0 %collective-permute-start.1 = (f32[12,8,256]{2,1,0:T(8,128)S(1)}, f32[12,8,256]{2,1,0:T(8,128)S(1)}, u32[]{:S(2)}, u32[]{:S(2)}) collective-permute-start(f32[12,8,256]{2,1,0:T(8,128)S(1)} %get-tuple-element.23.mine), channel_id=1, source_target_pairs={{0,1},{1,0},{2,3},{3,2},{4,5},{5,4},{6,7},{7,6},{8,9},{9,8},{10,11... | collective-permute-start | bytes 294920 | tf_op jit(solution)/shard_map/ppermute | solution.py:614
  22.7 3.4 %copy-start.1 = (bf16[2,12,8,256]{3,2,1,0:T(8,128)(2,1)S(1)}, bf16[2,12,8,256]{3,2,1,0:T(8,128)(2,1)}, u32[]{:S(2)}) copy-start(bf16[2,12,8,256]{3,2,1,0:T(8,128)(2,1)} %observed.3) | copy-start | bytes 294916
  24.3 4.7 %collective-permute-start.2 = (f32[12,8,256]{2,1,0:T(8,128)S(1)}, f32[12,8,256]{2,1,0:T(8,128)S(1)}, u32[]{:S(2)}, u32[]{:S(2)}) collective-permute-start(f32[12,8,256]{2,1,0:T(8,128)S(1)} %get-tuple-element.29.mine), channel_id=1, source_target_pairs={{0,1},{1,0},{2,3},{3,2},{4,5},{5,4},{6,7},{7,6},{8,9},{9,8},{10,11... | collective-permute-start | bytes 294920 | tf_op jit(solution)/shard_map/ppermute | solution.py:614
  31.4 1.3 %collective-permute-start.3 = (f32[2,64,128]{2,1,0:T(8,128)S(1)}, f32[2,64,128]{2,1,0:T(8,128)S(1)}, u32[]{:S(2)}, u32[]{:S(2)}) collective-permute-start(f32[2,64,128]{2,1,0:T(8,128)S(1)} %get-tuple-element.34), channel_id=1, source_target_pairs={{0,2},{2,0},{4,6},{6,4},{8,10},{10,8},{12,14},{14,12},{16,18},{18,... | collective-permute-start | bytes 196616 | tf_op jit(solution)/shard_map/ppermute | solution.py:614

commit v2 on v0

--- a/solution.py
+++ b/solution.py
@@ -117,6 +117,12 @@
     return jnp.where(low, first, turn(second, 4)), jnp.where(low, turn(first, 4), second)
 
 
+def add_all(sums, values):
+    if sums is None:
+        return values
+    return [v if total is None else total + v for total, v in zip(sums, values)]
+
+
 def halves(value):
     high = value.astype(jnp.bfloat16)
     return high, (value - high.astype(jnp.float32)).astype(jnp.bfloat16)
@@ -214,6 +220,7 @@
 
 
 PIECES = 6
+SPARE_ROWS = 8
 
 
 def block_of(meta, tile, side):
@@ -307,7 +314,9 @@
     for side, jones in enumerate((row_jones, col_jones)):
         found = [station_block(meta, near, far, tile, side) for tile in range(tiles)]
         for tile, made in enumerate(expand(found, side == 0)):
-            jones[tile, 0], jones[tile, 1] = made[:, :LANES], made[:, LANES:]
+            for half in range(2):
+                lanes = slice(half * LANES, (half + 1) * LANES)
+                jones[tile, half, : made.shape[0]] = made[:, lanes]
     models(0, narrow, row_jones, col_jones, model, paired, weight)
 
 
@@ -332,14 +341,14 @@
                 weight[k, 3 * x + 2, :, lanes] = z_re + z_im
         return 0
 
-    lax.fori_loop(0, directions, weigh, 0, unroll=2)
+    lax.fori_loop(0, directions, weigh, 0, unroll=8)
 
     def add_samples(step, _):
         lanes = half_lanes(step % 2)
         first = step // 2 * CHUNK
         zero = jnp.zeros((8, LANES), jnp.float32)
         low = component(zero) < 4
-        sums = [[zero] * CHUNK for n in range(12)]
+        sums = [None] * 12
         for k in range(directions):
             parts = []
             for i in range(CHUNK):
@@ -350,7 +359,7 @@
                 parts.append((real + imag, real, imag))
             for n in range(12):
                 w = weight[k, n, :, lanes]
-                sums[n] = [sums[n][i] + w * parts[i][n % 3] for i in range(CHUNK)]
+                sums[n] = add_all(sums[n], [w * parts[i][n % 3] for i in range(CHUNK)])
         for i in range(CHUNK):
             one, two, three = ([sums[3 * x + m][i] for x in range(4)] for m in range(3))
             real = fold([one[x] - three[x] for x in range(4)])
@@ -360,7 +369,7 @@
             model[place + 1, :, lanes] = jnp.where(low, turn(real, 4), imag)
         return 0
 
-    lax.fori_loop(0, 2 * pairs // CHUNK, add_samples, 0)
+    lax.fori_loop(0, 2 * pairs // CHUNK, add_samples, 0, unroll=4)
 
 
 def curvature_kernel(meta, near, far, moments, terms, masks, products):
@@ -376,7 +385,8 @@
         made = expand([station_products(packed) for packed in found], side == 0)
         for tile in range(tiles):
             for half in range(2):
-                products[tile, side, half] = made[tile][:, half * LANES : (half + 1) * LANES]
+                lanes = slice(half * LANES, (half + 1) * LANES)
+                products[tile, side, half, : made[tile].shape[0]] = made[tile][:, lanes]
 
     def combine(step, _):
         tile, group = step // (directions // 4), step % (directions // 4)
@@ -451,7 +461,7 @@
         half, lanes = step % 2, half_lanes(step % 2)
         first = step // 2 * CHUNK
         zero = jnp.zeros((8, LANES), jnp.float32)
-        sums = [[zero] * CHUNK for n in range(12)]
+        sums = [None] * 12
         for p in range(pairs):
             parts = []
             for i in range(CHUNK):
@@ -460,7 +470,7 @@
                 parts.append((real + imag, real, imag))
             for n in range(12):
                 r = turned[p, n, :, lanes]
-                sums[n] = [sums[n][i] + r * parts[i][n % 3] for i in range(CHUNK)]
+                sums[n] = add_all(sums[n], [r * parts[i][n % 3] for i in range(CHUNK)])
         bits = component(zero)
         real = bits < 4
         equal = (bits >> 1) & 1 == bits & 1
@@ -468,8 +478,8 @@
             k = first + i
             p_re, p_im = arranged(row_jones, tile, half, k, 2)
             q_re, q_im = arranged(col_jones, tile, half, k, 1)
-            row_sum = [zero, zero]
-            col_sum = [zero, zero]
+            row_sum = [None, None]
+            col_sum = [None, None]
             for x in range(4):
                 a, b = x // 2, x % 2
                 y_re = sums[3 * x][i] - sums[3 * x + 2][i]
@@ -477,8 +487,8 @@
                 y_re = y_re + turn(y_re, 4)
                 y_im = y_im + turn(y_im, 4)
                 one, two = jnp.where(real, y_re, y_im), jnp.where(real, -y_im, y_re)
-                row_sum[a] = row_sum[a] + (q_re[b] * one + q_im[b] * two)
-                col_sum[b] = col_sum[b] + (p_re[a] * one - p_im[a] * two)
+                (row_sum[a],) = add_all(row_sum[a : a + 1], [q_re[b] * one + q_im[b] * two])
+                (col_sum[b],) = add_all(col_sum[b : b + 1], [p_re[a] * one - p_im[a] * two])
             rows = pl.ds(pl.multiple_of(8 * k, 8), 8)
             g, h = row_sum
             g = jnp.where(equal, g, h) + flip(jnp.where(equal, h, g), 1)
@@ -488,7 +498,7 @@
             terms[1, rows, lanes] = g
         return 0
 
-    lax.fori_loop(0, 2 * directions // CHUNK, add_directions, 0)
+    lax.fori_loop(0, 2 * directions // CHUNK, add_directions, 0, unroll=4)
     return sent
 
 
@@ -636,7 +646,7 @@
     )
     far = swap_with(near, "tile", 1)
 
-    expanded = (tiles, 2, 4 * rows, LANES)
+    expanded = (tiles, 2, 4 * rows + SPARE_ROWS, LANES)
     of_tile = [(samples, 8, BASELINES), (directions, samples // 2, 2, 8, BASELINES)]
     narrow = pltpu.with_memory_space_constraint(narrow, pltpu.VMEM)
     weight = memory(directions, 12, 8, BASELINES)
@@ -677,7 +687,7 @@
         [meta, near, far, moments],
         [],
         [(2, tiles, 2 * directions, BASELINES), (tiles, 1 + flags.shape[1], 8, BASELINES)],
-        [memory(tiles, 2, 2, 4 * directions, LANES)],
+        [memory(tiles, 2, 2, 4 * directions + SPARE_ROWS, LANES)],
         cost=pl.CostEstimate(
             flops=coherency.size, bytes_accessed=coherency.size, transcendentals=0
         ),
@@ -782,7 +792,7 @@
     def run(coherency, observed, flags, tile_map, jones):
         owned = jones.shape[2] // mesh.shape["tile"]
         directions = jones.shape[0] // mesh.shape["dir"]
-        fits = owned == 2 * SB and directions % 12 == 0
+        fits = owned == 2 * SB and directions == 24
         paired = mesh.shape["dir"] == 2 and mesh.shape["tile"] == 16
         paired = paired and coherency.shape[0] == 2 * mesh.shape["tile"]
         chosen = body_kernels if fits and paired else body

time: 46.2 us -> 45.8 us (level)
  Pallas kernels: 16.1 us -> 15.5 us
    pallas_call x7, Pallas kernels: 15.4 us -> 14.7 us  [call(): pl.pallas_call(kernel, in_specs=[place(space) for space in spaces], out_s...]
  transfers between devices with their start and end apart: 5 -> 5, of which waited for: 4 -> 4; matrix products, arithmetic and copies ran while one was open for 0% -> 0% of each run, Pallas kernels for 20% -> 19%
where the time goes in v2:
time: 45.8 us; the launch traced here: 45.5 us
  Pallas kernels  15.5 us (34%)
  blocking collectives  12.2 us (27%)
  starting transfers between devices  9.52 us (21%)
  waiting for transfers between devices  7.43 us (16%)
  between operations  0.72 us (2%)
    pallas_call x7, Pallas kernels, call(): pl.pallas_call(kernel, in_specs=[place(space) for space in spaces], out_s...  14.7 us
    all_to_all x1, blocking collectives, trade(): lax.all_to_all(slots, 'tile', 0, 0, axis_index_groups=groups, tiled=True)  12.2 us
    all_to_all x1, starting transfers between devices, trade(): lax.all_to_all(slots, 'tile', 0, 0, axis_index_groups=groups, tiled=True)  7.29 us
    ppermute x4, waiting for transfers between devices, swap_with(): lax.ppermute(value, axis, [(place, place ^ mask) for place in range(size)])  4.16 us
    all_to_all x1, waiting for transfers between devices, trade(): lax.all_to_all(slots, 'tile', 0, 0, axis_index_groups=groups, tiled=True)  3.27 us
    ppermute x4, starting transfers between devices, swap_with(): lax.ppermute(value, axis, [(place, place ^ mask) for place in range(size)])  2.23 us
  transfers between devices with their start and end apart: 5, of which 4 were waited for; matrix products, arithmetic and copies ran while one was open for 0% of the time, Pallas kernels for 19%

profile of v2, /device:TPU:0, one launch (start us, length us, event | category | flops | bytes accessed | tf_op | source)
XLA Modules:
  0.0 45.5 jit_solution(14796170958357822105)
XLA Ops:
  0.6 0.0 copy-start.2
  0.6 0.0 copy-start.3
  0.7 1.8 %shard_map.76 = f32[8,48,128]{2,1,0:T(8,128)} custom-call(f32[24,8,32]{2,1,0:T(8,128)} %jones_in_hbm.1), custom_call_target="tpu_custom_call" | custom-call | tf_op jit(solution)/shard_map/pallas_call | solution.py:573
  2.4 7.3 %all-to-all-start = ((f32[8,48,128]{2,1,0:T(8,128)}), f32[8,48,128]{2,1,0:T(8,128)S(1)}, u32[]{:S(2)}, u32[]{:S(2)}) async-start(f32[8,48,128]{2,1,0:T(8,128)} %shard_map.76), calls=%async_computation | async-start | bytes 393216 | tf_op jit(solution)/shard_map/all_to_all | solution.py:596
  9.7 4.6 %shard_map.77 = (f32[2,4,192,256]{3,2,1,0:T(8,128)}, bf16[2,24,6,16,256]{4,3,2,1,0:T(8,128)(2,1)S(1)}) custom-call(s32[2,3]{1,0:T(2,128)} %flags_in_hbm.1, bf16[2,24,12,8,256]{4,3,2,1,0:T(8,128)(2,1)} %source.1), custom_call_target="tpu_custom_call" | custom-call | flops 11796480 | bytes 4718592 | tf_op jit(solution)/shard_map/pallas_call | solution.py:573
  14.3 0.1 pad_add_fusion.1
  14.4 3.3 %all-to-all-done.near = f32[8,48,128]{2,1,0:T(8,128)S(1)} async-done(((f32[8,48,128]{2,1,0:T(8,128)}), f32[8,48,128]{2,1,0:T(8,128)S(1)}, u32[]{:S(2)}, u32[]{:S(2)}) %all-to-all-start) | async-done | bytes 196640 | tf_op jit(solution)/shard_map/all_to_all | solution.py:596
  17.7 0.0 collective-permute-start
  17.7 0.0 copy-done.2
  17.7 0.0 copy-done.3
  17.7 0.1 pad_add_fusion.meta.meta_in_vmem
  17.7 1.4 %collective-permute-done.far = f32[8,48,128]{2,1,0:T(8,128)S(1)} collective-permute-done((f32[8,48,128]{2,1,0:T(8,128)S(1)}, f32[8,48,128]{2,1,0:T(8,128)S(1)}, u32[]{:S(2)}, u32[]{:S(2)}) %collective-permute-start) | collective-permute-done | bytes 196640 | tf_op jit(solution)/shard_map/ppermute | solution.py:590
  19.1 0.0 copy-start
  19.1 2.0 %shard_map.79 = (f32[12,8,256]{2,1,0:T(8,128)S(1)}, f32[2,2,200,128]{3,2,1,0:T(8,128)S(1)}, f32[2,2,200,128]{3,2,1,0:T(8,128)S(1)}, f32[24,6,2,8,256]{4,3,2,1,0:T(8,128)S(1)}) custom-call(s32[2,7]{1,0:T(2,128)S(1)} %pad_add_fusion.meta.meta_in_vmem, f32[8,48,128]{2,1,0:T(8,128)S(1)} %all-to-all-done.near, f32[8,48,128]{2,1,0:T(8,128)S(1)} %collective-permute-done.far, ...), custom_call_target="tpu_custom_call" | custom-call | tf_op jit(solution)/shard_map/pallas_call | solution.py:573
  21.1 1.6 %collective-permute-start.1 = (f32[12,8,256]{2,1,0:T(8,128)S(1)}, f32[12,8,256]{2,1,0:T(8,128)S(1)}, u32[]{:S(2)}, u32[]{:S(2)}) collective-permute-start(f32[12,8,256]{2,1,0:T(8,128)S(1)} %get-tuple-element.23.mine), channel_id=1, source_target_pairs={{0,1},{1,0},{2,3},{3,2},{4,5},{5,4},{6,7},{7,6},{8,9},{9,8},{10,11... | collective-permute-start | bytes 294920 | tf_op jit(solution)/shard_map/ppermute | solution.py:590
  22.7 0.0 copy-start.1
  22.7 1.5 %shard_map.81 = (f32[12,8,256]{2,1,0:T(8,128)S(1)}, f32[24,6,2,8,256]{4,3,2,1,0:T(8,128)S(1)}) custom-call(bf16[2,24,6,16,256]{4,3,2,1,0:T(8,128)(2,1)S(1)} %get-tuple-element.22.narrow, f32[2,2,200,128]{3,2,1,0:T(8,128)S(1)} %get-tuple-element.24.row_jones, f32[2,2,200,128]{3,2,1,0:T(8,128)S(1)} %get-tuple-element.25.col_jones), custom_call_target="tpu_custom_call" | custom-call | tf_op jit(solution)/shard_map/pallas_call | solution.py:573
  24.2 0.6 %collective-permute-start.2 = (f32[12,8,256]{2,1,0:T(8,128)S(1)}, f32[12,8,256]{2,1,0:T(8,128)S(1)}, u32[]{:S(2)}, u32[]{:S(2)}) collective-permute-start(f32[12,8,256]{2,1,0:T(8,128)S(1)} %get-tuple-element.29.mine), channel_id=1, source_target_pairs={{0,1},{1,0},{2,3},{3,2},{4,5},{5,4},{6,7},{7,6},{8,9},{9,8},{10,11... | collective-permute-start | bytes 294920 | tf_op jit(solution)/shard_map/ppermute | solution.py:590
  24.8 0.0 copy-done
  24.8 1.2 %shard_map.78 = (f32[2,2,48,256]{3,2,1,0:T(8,128)S(1)}, f32[2,4,8,256]{3,2,1,0:T(8,128)S(1)}) custom-call(s32[2,7]{1,0:T(2,128)S(1)} %pad_add_fusion.meta.meta_in_vmem, f32[8,48,128]{2,1,0:T(8,128)S(1)} %all-to-all-done.near, f32[8,48,128]{2,1,0:T(8,128)S(1)} %collective-permute-done.far, f32[2,4,192,256]{3,2,1,0:T(8,128)S(1)} %copy-done), custom_call_target="tpu_custom_call" | custom-call | flops 1179648 | bytes 1179648 | tf_op jit(solution)/shard_map/pallas_call | solution.py:573
  26.0 0.0 collective-permute-done.1.other
  26.0 0.0 copy-done.1
  26.0 1.6 %shard_map.80 = (f32[2,12,8,128]{3,2,1,0:T(8,128)}, f32[2,192,256]{2,1,0:T(8,128)S(1)}) custom-call(s32[2,7]{1,0:T(2,128)S(1)} %pad_add_fusion.meta.meta_in_vmem, f32[2,4,8,256]{3,2,1,0:T(8,128)S(1)} %get-tuple-element.21.masks, bf16[2,12,8,256]{3,2,1,0:T(8,128)(2,1)S(1)} %copy-done.1, f32[12,8,256]{2,1,0:T(8,128)S(1)} %get-tuple-element.23.mine, ...), custom_call_target="tpu_custom_call" | custom-call | tf_op jit(solution)/shard_map/pallas_call | solution.py:573
  27.6 1.2 %collective-permute-done.2.other = f32[12,8,256]{2,1,0:T(8,128)S(1)} collective-permute-done((f32[12,8,256]{2,1,0:T(8,128)S(1)}, f32[12,8,256]{2,1,0:T(8,128)S(1)}, u32[]{:S(2)}, u32[]{:S(2)}) %collective-permute-start.2) | collective-permute-done | bytes 98336 | tf_op jit(solution)/shard_map/ppermute | solution.py:590
  28.8 2.1 %shard_map.82 = (f32[2,12,8,128]{3,2,1,0:T(8,128)}, f32[8,64,128]{2,1,0:T(8,128)S(1)}, f32[8,64,128]{2,1,0:T(8,128)S(1)}) custom-call(s32[2,7]{1,0:T(2,128)S(1)} %pad_add_fusion.meta.meta_in_vmem, f32[2,192,256]{2,1,0:T(8,128)S(1)} %get-tuple-element.27.first_terms, ...), custom_call_target="tpu_custom_call", output_to_operand_aliasing={{0}: (10, {})} | custom-call | tf_op jit(solution)/shard_map/pallas_call | solution.py:573
  31.0 0.1 collective-permute-start.3
  31.1 1.5 %collective-permute-done.3 = f32[8,64,128]{2,1,0:T(8,128)S(1)} collective-permute-done((f32[8,64,128]{2,1,0:T(8,128)S(1)}, f32[8,64,128]{2,1,0:T(8,128)S(1)}, u32[]{:S(2)}, u32[]{:S(2)}) %collective-permute-start.3) | collective-permute-done | bytes 262176 | tf_op jit(solution)/shard_map/ppermute | solution.py:590
  32.6 12.2 %all_to_all.10.parts = f32[8,64,128]{2,1,0:T(8,128)S(1)} all-to-all(f32[8,64,128]{2,1,0:T(8,128)S(1)} %add.3), channel_id=1, replica_groups={{0,4,8,12,16,20,24,28},{2,6,10,14,18,22,26,30},{1,5,9,13,17,21,25,29},{..., dimensions={0} | all-to-all | bytes 524288 | tf_op jit(solution)/shard_map/all_to_all | solution.py:596
  44.8 0.7 %shard_map.83 = (f32[24,8,32]{2,1,0:T(8,128)}, f32[24,2,32]{2,1,0:T(2,128)}) custom-call(f32[8,64,128]{2,1,0:T(8,128)S(1)} %all_to_all.10.parts), custom_call_target="tpu_custom_call" | custom-call | tf_op jit(solution)/shard_map/pallas_call | solution.py:723
  (1 shorter events, 0.0 us)
Async XLA Ops:
  0.6 17.0 %copy-start.2 = (s32[2,3]{1,0:T(2,128)S(1)}, s32[2,3]{1,0:T(2,128)}, u32[]{:S(2)}) copy-start(s32[2,3]{1,0:T(2,128)} %flags_in_hbm.1) | copy-start | bytes 76
  0.6 17.0 %copy-start.3 = (s32[2,2]{1,0:T(2,128)S(1)}, s32[2,2]{1,0:T(2,128)}, u32[]{:S(2)}) copy-start(s32[2,2]{1,0:T(2,128)} %param.8) | copy-start | bytes 52
  2.4 15.2 %all-to-all-start = ((f32[8,48,128]{2,1,0:T(8,128)}), f32[8,48,128]{2,1,0:T(8,128)S(1)}, u32[]{:S(2)}, u32[]{:S(2)}) async-start(f32[8,48,128]{2,1,0:T(8,128)} %shard_map.76), calls=%async_computation | async-start | bytes 393216 | tf_op jit(solution)/shard_map/all_to_all | solution.py:596
  17.7 1.4 %collective-permute-start = (f32[8,48,128]{2,1,0:T(8,128)S(1)}, f32[8,48,128]{2,1,0:T(8,128)S(1)}, u32[]{:S(2)}, u32[]{:S(2)}) collective-permute-start(f32[8,48,128]{2,1,0:T(8,128)S(1)} %all-to-all-done.near), channel_id=1, source_target_pairs={{0,2},{2,0},{4,6},{6,4},{8,10},{10,8},{12,14},{14,12},{16,18},{18,... | collective-permute-start | bytes 589832 | tf_op jit(solution)/shard_map/ppermute | solution.py:590
  19.1 5.7 %copy-start = (f32[2,4,192,256]{3,2,1,0:T(8,128)S(1)}, f32[2,4,192,256]{3,2,1,0:T(8,128)}, u32[]{:S(2)}) copy-start(f32[2,4,192,256]{3,2,1,0:T(8,128)} %get-tuple-element.20.moments) | copy-start | bytes 4718596
  21.1 4.9 %collective-permute-start.1 = (f32[12,8,256]{2,1,0:T(8,128)S(1)}, f32[12,8,256]{2,1,0:T(8,128)S(1)}, u32[]{:S(2)}, u32[]{:S(2)}) collective-permute-start(f32[12,8,256]{2,1,0:T(8,128)S(1)} %get-tuple-element.23.mine), channel_id=1, source_target_pairs={{0,1},{1,0},{2,3},{3,2},{4,5},{5,4},{6,7},{7,6},{8,9},{9,8},{10,11... | collective-permute-start | bytes 294920 | tf_op jit(solution)/shard_map/ppermute | solution.py:590
  22.7 3.3 %copy-start.1 = (bf16[2,12,8,256]{3,2,1,0:T(8,128)(2,1)S(1)}, bf16[2,12,8,256]{3,2,1,0:T(8,128)(2,1)}, u32[]{:S(2)}) copy-start(bf16[2,12,8,256]{3,2,1,0:T(8,128)(2,1)} %observed.3) | copy-start | bytes 294916
  24.2 4.7 %collective-permute-start.2 = (f32[12,8,256]{2,1,0:T(8,128)S(1)}, f32[12,8,256]{2,1,0:T(8,128)S(1)}, u32[]{:S(2)}, u32[]{:S(2)}) collective-permute-start(f32[12,8,256]{2,1,0:T(8,128)S(1)} %get-tuple-element.29.mine), channel_id=1, source_target_pairs={{0,1},{1,0},{2,3},{3,2},{4,5},{5,4},{6,7},{7,6},{8,9},{9,8},{10,11... | collective-permute-start | bytes 294920 | tf_op jit(solution)/shard_map/ppermute | solution.py:590
  31.0 1.6 %collective-permute-start.3 = (f32[8,64,128]{2,1,0:T(8,128)S(1)}, f32[8,64,128]{2,1,0:T(8,128)S(1)}, u32[]{:S(2)}, u32[]{:S(2)}) collective-permute-start(f32[8,64,128]{2,1,0:T(8,128)S(1)} %get-tuple-element.34), channel_id=1, source_target_pairs={{0,2},{2,0},{4,6},{6,4},{8,10},{10,8},{12,14},{14,12},{16,18},{18,... | collective-permute-start | bytes 786440 | tf_op jit(solution)/shard_map/ppermute | solution.py:590

commit v3 on v2

--- a/solution.py
+++ b/solution.py
@@ -184,22 +184,17 @@
     return jnp.where((baseline // SB < baseline % SB) | above, 1.0, 0.0).astype(jnp.float32)
 
 
-def pack_kernel(jones_in_hbm, slots, jones, packed, in_semaphore, semaphores):
-    copy = pltpu.make_async_copy(jones_in_hbm, jones, in_semaphore)
+def pack_kernel(jones_in_hbm, packed, jones, semaphore):
+    copy = pltpu.make_async_copy(jones_in_hbm, jones, semaphore)
     copy.start()
     copy.wait()
     each = jones.shape[0] // 4
-    rows = packed.shape[0]
-    packed[...] = jnp.concatenate(
+    rows = packed.shape[1]
+    made = jnp.concatenate(
         [jones[g * each : (g + 1) * each].reshape(rows, 2 * SB) for g in range(4)], axis=1
     )
-    copies = [
-        pltpu.make_async_copy(packed, slots.at[n], semaphores.at[n]) for n in range(slots.shape[0])
-    ]
-    for copy in copies:
-        copy.start()
-    for copy in copies:
-        copy.wait()
+    for copy in range(packed.shape[0]):
+        packed[copy] = made
 
 
 def entry(meta, row, column, shape=(8, LANES)):
@@ -422,14 +417,23 @@
                 terms[side, tile, place, lanes] = mask[:, lanes] * found[side]
         return 0
 
-    lax.fori_loop(0, tiles * directions // 4, combine, 0)
-
-
-def add_to_owner(meta, near, far, block, part):
+    lax.fori_loop(0, tiles * directions // 4, combine, 0, unroll=3)
+
+
+def add_to_owner(meta, near, far, block, rows, part):
     owner = block // 2
     own_core = jnp.where(owner % 2 == meta[0, 0] % 2, 1.0, 0.0)
-    near[owner // 2] = near[owner // 2] + own_core * part
-    far[owner // 2] = far[owner // 2] + (1.0 - own_core) * part
+    near[owner // 2, rows] = near[owner // 2, rows] + own_core * part
+    far[owner // 2, rows] = far[owner // 2, rows] + (1.0 - own_core) * part
+
+
+def gradient_block(sums, half, side):
+    part = to_lanes(jnp.split(sums, 4, axis=0), half).reshape(-1, 8, LANES)
+    if side == 0:
+        part = transpose_matrix(part)
+    else:
+        part = jnp.where(component(part) < 4, part, -part)
+    return part.reshape(-1, LANES)
 
 
 def add_gradient_terms(
@@ -503,51 +507,53 @@
 
 
 def first_gradient_kernel(
-    meta, masks, observed, mine, other, row_jones, col_jones, paired,
-    residual_out, terms, residual, turned, semaphore,
+    meta_in_vmem, curvature_terms, masks, observed, mine, other, row_jones, col_jones, paired,
+    residual_out, near, far, terms, residual, turned, semaphore, meta, meta_semaphore,
 ):
+    meta_copy = pltpu.make_async_copy(meta_in_vmem, meta, meta_semaphore)
+    meta_copy.start()
     sent = add_gradient_terms(
-        0, meta, masks, observed, mine, other, row_jones, col_jones, paired,
+        0, meta_in_vmem, masks, observed, mine, other, row_jones, col_jones, paired,
         residual_out, terms, residual, turned, semaphore,
     )
+    near[...] = jnp.zeros_like(near)
+    far[...] = jnp.zeros_like(far)
+    meta_copy.wait()
+    tiles, directions = curvature_terms.shape[1], paired.shape[0]
+    rows, few = 8 * directions, 2 * directions
+    for side, blocks in enumerate(sides(meta, tiles)):
+        stack = [terms[side], *(curvature_terms[side, tile] for tile in range(tiles))]
+        sums = station_sums(jnp.concatenate(stack, axis=0), side == 0)
+        part = gradient_block(sums[:rows], blocks[0] % 2, side)
+        add_to_owner(meta, near, far, blocks[0], slice(0, few), part)
+        for tile, block in enumerate(blocks):
+            start = rows + tile * few
+            groups = jnp.split(sums[start : start + few], directions // 4, axis=0)
+            chosen = [groups[n : n + 4] for n in range(0, len(groups), 4)]
+            made = [to_lanes(parts, block % 2) for parts in chosen]
+            part = jnp.concatenate(made, axis=0)
+            add_to_owner(meta, near, far, block, slice(few, None), part)
     sent.wait()
 
 
 def last_gradient_kernel(
-    tiles, meta_in_vmem, first_terms, curvature_terms,
+    tiles, meta_in_vmem, near_before, far_before,
     masks, observed, mine, other, row_jones, col_jones, paired,
     residual_before, residual_out, near, far, terms, residual, turned, semaphore,
     meta, meta_semaphore,
 ):
-    del residual_before
+    del residual_before, near_before, far_before
     meta_copy = pltpu.make_async_copy(meta_in_vmem, meta, meta_semaphore)
     meta_copy.start()
     sent = add_gradient_terms(
         tiles - 1, meta_in_vmem, masks, observed, mine, other, row_jones, col_jones, paired,
         residual_out, terms, residual, turned, semaphore,
     )
-    near[...] = jnp.zeros_like(near)
-    far[...] = jnp.zeros_like(far)
     meta_copy.wait()
-    directions = paired.shape[0]
-    rows, few = 8 * directions, 2 * directions
-    for side, blocks in enumerate(sides(meta, tiles)):
-        stack = [first_terms[side], terms[side]]
-        stack.extend(curvature_terms[side, tile] for tile in range(tiles))
-        sums = station_sums(jnp.concatenate(stack, axis=0), side == 0)
-        for tile, block in enumerate(blocks):
-            half = block % 2
-            part = to_lanes(jnp.split(sums[tile * rows : (tile + 1) * rows], 4, axis=0), half)
-            part = part.reshape(-1, 8, LANES)
-            if side == 0:
-                part = transpose_matrix(part)
-            else:
-                part = jnp.where(component(part) < 4, part, -part)
-            start = tiles * rows + tile * few
-            groups = jnp.split(sums[start : start + few], directions // 4, axis=0)
-            chosen = [groups[n : n + 4] for n in range(0, len(groups), 4)]
-            made = [part.reshape(-1, LANES), *(to_lanes(parts, half) for parts in chosen)]
-            add_to_owner(meta, near, far, block, jnp.concatenate(made, axis=0))
+    for side in range(2):
+        block = block_of(meta, tiles - 1, side)
+        part = gradient_block(station_sums(terms[side], side == 0), block % 2, side)
+        add_to_owner(meta, near, far, block, slice(0, part.shape[0]), part)
     sent.wait()
 
 
@@ -614,14 +620,8 @@
         [],
         [],
         [jones],
-        [],
-        [
-            memory(*jones.shape),
-            memory(rows, LANES),
-            pltpu.SemaphoreType.DMA,
-            pltpu.SemaphoreType.DMA((chips,)),
-        ],
         [(chips, rows, LANES)],
+        [memory(*jones.shape), pltpu.SemaphoreType.DMA],
     )
     near = trade(packed)
     narrow = (tiles, directions, samples // 2, 16, BASELINES)
@@ -692,30 +692,31 @@
             flops=coherency.size, bytes_accessed=coherency.size, transcendentals=0
         ),
     )
-    residual, first_terms = call(
+    scratch = [
+        memory(*terms),
+        *scratch,
+        pltpu.SMEM(meta.shape, meta.dtype),
+        pltpu.SemaphoreType.DMA,
+    ]
+    slots = (chips, rows + extra, LANES)
+    residual, near, far = call(
         first_gradient_kernel,
         [],
-        [meta, masks, observed, *first],
-        [],
-        [terms],
+        [meta, curvature_terms, masks, observed, *first],
+        [],
+        [slots, slots],
         scratch,
         [residual_shape],
     )
-    slots = (chips, rows + extra, LANES)
     residual, near, far = call(
         functools.partial(last_gradient_kernel, tiles),
         [],
-        [meta, first_terms, curvature_terms, masks, observed, *last],
+        [meta, near, far, masks, observed, *last],
         [residual],
         [slots, slots],
-        [
-            memory(*terms),
-            *scratch,
-            pltpu.SMEM(meta.shape, meta.dtype),
-            pltpu.SemaphoreType.DMA,
-        ],
+        scratch,
         [residual_shape],
-        {10: 0},
+        {10: 0, 1: 1, 2: 2},
     )
     parts = trade(near + swap_with(far, "tile", 1))
     directions, _, owned = jones.shape

time: 45.8 us -> 45.6 us (level)
  transfers between devices with their start and end apart: 5 -> 5, of which waited for: 4 -> 5; matrix products, arithmetic and copies ran while one was open for 0% -> 0% of each run, Pallas kernels for 19% -> 20%
where the time goes in v3:
time: 45.6 us; the launch traced here: 45.3 us
  Pallas kernels  15.5 us (34%)
  blocking collectives  12.2 us (27%)
  starting transfers between devices  9.52 us (21%)
  waiting for transfers between devices  7.18 us (16%)
  between operations  0.72 us (2%)
    pallas_call x7, Pallas kernels, call(): pl.pallas_call(kernel, in_specs=[place(space) for space in spaces], out_s...  14.7 us
    all_to_all x1, blocking collectives, trade(): lax.all_to_all(slots, 'tile', 0, 0, axis_index_groups=groups, tiled=True)  12.2 us
    all_to_all x1, starting transfers between devices, trade(): lax.all_to_all(slots, 'tile', 0, 0, axis_index_groups=groups, tiled=True)  7.29 us
    ppermute x4, waiting for transfers between devices, swap_with(): lax.ppermute(value, axis, [(place, place ^ mask) for place in range(size)])  3.91 us
    all_to_all x1, waiting for transfers between devices, trade(): lax.all_to_all(slots, 'tile', 0, 0, axis_index_groups=groups, tiled=True)  3.27 us
    ppermute x4, starting transfers between devices, swap_with(): lax.ppermute(value, axis, [(place, place ^ mask) for place in range(size)])  2.23 us
  transfers between devices with their start and end apart: 5, of which 5 were waited for; matrix products, arithmetic and copies ran while one was open for 0% of the time, Pallas kernels for 20%

profile of v3, /device:TPU:0, one launch (start us, length us, event | category | flops | bytes accessed | tf_op | source)
XLA Modules:
  0.0 45.3 jit_solution(915540368026953151)
XLA Ops:
  0.6 0.0 copy-start.2
  0.6 0.0 copy-start.3
  0.7 1.7 %shard_map.76 = f32[8,48,128]{2,1,0:T(8,128)} custom-call(f32[24,8,32]{2,1,0:T(8,128)} %jones_in_hbm.1), custom_call_target="tpu_custom_call" | custom-call | tf_op jit(solution)/shard_map/pallas_call | solution.py:579
  2.3 7.3 %all-to-all-start = ((f32[8,48,128]{2,1,0:T(8,128)}), f32[8,48,128]{2,1,0:T(8,128)S(1)}, u32[]{:S(2)}, u32[]{:S(2)}) async-start(f32[8,48,128]{2,1,0:T(8,128)} %shard_map.76), calls=%async_computation | async-start | bytes 393216 | tf_op jit(solution)/shard_map/all_to_all | solution.py:602
  9.6 4.6 %shard_map.77 = (f32[2,4,192,256]{3,2,1,0:T(8,128)}, bf16[2,24,6,16,256]{4,3,2,1,0:T(8,128)(2,1)S(1)}) custom-call(s32[2,3]{1,0:T(2,128)} %flags_in_hbm.1, bf16[2,24,12,8,256]{4,3,2,1,0:T(8,128)(2,1)} %source.1), custom_call_target="tpu_custom_call" | custom-call | flops 11796480 | bytes 4718592 | tf_op jit(solution)/shard_map/pallas_call | solution.py:579
  14.2 0.1 pad_add_fusion.1
  14.3 3.3 %all-to-all-done.near = f32[8,48,128]{2,1,0:T(8,128)S(1)} async-done(((f32[8,48,128]{2,1,0:T(8,128)}), f32[8,48,128]{2,1,0:T(8,128)S(1)}, u32[]{:S(2)}, u32[]{:S(2)}) %all-to-all-start) | async-done | bytes 196640 | tf_op jit(solution)/shard_map/all_to_all | solution.py:602
  17.6 0.0 collective-permute-start
  17.6 0.0 copy-done.2
  17.6 0.0 copy-done.3
  17.6 0.1 pad_add_fusion.meta.meta_in_vmem
  17.7 1.4 %collective-permute-done.far = f32[8,48,128]{2,1,0:T(8,128)S(1)} collective-permute-done((f32[8,48,128]{2,1,0:T(8,128)S(1)}, f32[8,48,128]{2,1,0:T(8,128)S(1)}, u32[]{:S(2)}, u32[]{:S(2)}) %collective-permute-start) | collective-permute-done | bytes 196640 | tf_op jit(solution)/shard_map/ppermute | solution.py:596
  19.0 0.0 copy-start
  19.0 2.0 %shard_map.79 = (f32[12,8,256]{2,1,0:T(8,128)S(1)}, f32[2,2,200,128]{3,2,1,0:T(8,128)S(1)}, f32[2,2,200,128]{3,2,1,0:T(8,128)S(1)}, f32[24,6,2,8,256]{4,3,2,1,0:T(8,128)S(1)}) custom-call(s32[2,7]{1,0:T(2,128)S(1)} %pad_add_fusion.meta.meta_in_vmem, f32[8,48,128]{2,1,0:T(8,128)S(1)} %all-to-all-done.near, f32[8,48,128]{2,1,0:T(8,128)S(1)} %collective-permute-done.far, ...), custom_call_target="tpu_custom_call" | custom-call | tf_op jit(solution)/shard_map/pallas_call | solution.py:579
  21.0 1.6 %collective-permute-start.1 = (f32[12,8,256]{2,1,0:T(8,128)S(1)}, f32[12,8,256]{2,1,0:T(8,128)S(1)}, u32[]{:S(2)}, u32[]{:S(2)}) collective-permute-start(f32[12,8,256]{2,1,0:T(8,128)S(1)} %get-tuple-element.25.mine), channel_id=1, source_target_pairs={{0,1},{1,0},{2,3},{3,2},{4,5},{5,4},{6,7},{7,6},{8,9},{9,8},{10,11... | collective-permute-start | bytes 294920 | tf_op jit(solution)/shard_map/ppermute | solution.py:596
  22.6 0.0 copy-start.1
  22.6 1.5 %shard_map.81 = (f32[12,8,256]{2,1,0:T(8,128)S(1)}, f32[24,6,2,8,256]{4,3,2,1,0:T(8,128)S(1)}) custom-call(bf16[2,24,6,16,256]{4,3,2,1,0:T(8,128)(2,1)S(1)} %get-tuple-element.24.narrow, f32[2,2,200,128]{3,2,1,0:T(8,128)S(1)} %get-tuple-element.26.row_jones, f32[2,2,200,128]{3,2,1,0:T(8,128)S(1)} %get-tuple-element.27.col_jones), custom_call_target="tpu_custom_call" | custom-call | tf_op jit(solution)/shard_map/pallas_call | solution.py:579
  24.1 0.6 %collective-permute-start.2 = (f32[12,8,256]{2,1,0:T(8,128)S(1)}, f32[12,8,256]{2,1,0:T(8,128)S(1)}, u32[]{:S(2)}, u32[]{:S(2)}) collective-permute-start(f32[12,8,256]{2,1,0:T(8,128)S(1)} %get-tuple-element.31.mine), channel_id=1, source_target_pairs={{0,1},{1,0},{2,3},{3,2},{4,5},{5,4},{6,7},{7,6},{8,9},{9,8},{10,11... | collective-permute-start | bytes 294920 | tf_op jit(solution)/shard_map/ppermute | solution.py:596
  24.7 0.0 copy-done
  24.7 1.0 %shard_map.78 = (f32[2,2,48,256]{3,2,1,0:T(8,128)S(1)}, f32[2,4,8,256]{3,2,1,0:T(8,128)S(1)}) custom-call(s32[2,7]{1,0:T(2,128)S(1)} %pad_add_fusion.meta.meta_in_vmem, f32[8,48,128]{2,1,0:T(8,128)S(1)} %all-to-all-done.near, f32[8,48,128]{2,1,0:T(8,128)S(1)} %collective-permute-done.far, f32[2,4,192,256]{3,2,1,0:T(8,128)S(1)} %copy-done), custom_call_target="tpu_custom_call" | custom-call | flops 1179648 | bytes 1179648 | tf_op jit(solution)/shard_map/pallas_call | solution.py:579
  25.7 0.2 collective-permute-done.1.other
  25.9 0.0 copy-done.1
  25.9 2.0 %shard_map.80 = (f32[2,12,8,128]{3,2,1,0:T(8,128)}, f32[8,64,128]{2,1,0:T(8,128)S(1)}, f32[8,64,128]{2,1,0:T(8,128)S(1)}) custom-call(s32[2,7]{1,0:T(2,128)S(1)} %pad_add_fusion.meta.meta_in_vmem, f32[2,2,48,256]{3,2,1,0:T(8,128)S(1)} %get-tuple-element.22.curvature_terms, f32[2,4,8,256]{3,2,1,0:T(8,128)S(1)} %get-tuple-element.23.masks, ...), custom_call_target="tpu_custom_call" | custom-call | tf_op jit(solution)/shard_map/pallas_call | solution.py:579
  28.0 0.8 %collective-permute-done.2.other = f32[12,8,256]{2,1,0:T(8,128)S(1)} collective-permute-done((f32[12,8,256]{2,1,0:T(8,128)S(1)}, f32[12,8,256]{2,1,0:T(8,128)S(1)}, u32[]{:S(2)}, u32[]{:S(2)}) %collective-permute-start.2) | collective-permute-done | bytes 98336 | tf_op jit(solution)/shard_map/ppermute | solution.py:596
  28.8 2.0 %shard_map.82 = (f32[2,12,8,128]{3,2,1,0:T(8,128)}, f32[8,64,128]{2,1,0:T(8,128)S(1)}, f32[8,64,128]{2,1,0:T(8,128)S(1)}) custom-call(s32[2,7]{1,0:T(2,128)S(1)} %pad_add_fusion.meta.meta_in_vmem, f32[8,64,128]{2,1,0:T(8,128)S(1)} %get-tuple-element.29.near_before, ...), custom_call_target="tpu_custom_call", output_to_operand_aliasing={{0}: (10, {}), {1}: (1, {}), {2}: (2, {})} | custom-call | tf_op jit(solution)/shard_map/pallas_call | solution.py:579
  30.7 0.1 collective-permute-start.3
  30.8 1.5 %collective-permute-done.3 = f32[8,64,128]{2,1,0:T(8,128)S(1)} collective-permute-done((f32[8,64,128]{2,1,0:T(8,128)S(1)}, f32[8,64,128]{2,1,0:T(8,128)S(1)}, u32[]{:S(2)}, u32[]{:S(2)}) %collective-permute-start.3) | collective-permute-done | bytes 262176 | tf_op jit(solution)/shard_map/ppermute | solution.py:596
  32.4 12.2 %all_to_all.10.parts = f32[8,64,128]{2,1,0:T(8,128)S(1)} all-to-all(f32[8,64,128]{2,1,0:T(8,128)S(1)} %add.3), channel_id=1, replica_groups={{0,4,8,12,16,20,24,28},{2,6,10,14,18,22,26,30},{1,5,9,13,17,21,25,29},{..., dimensions={0} | all-to-all | bytes 524288 | tf_op jit(solution)/shard_map/all_to_all | solution.py:602
  44.5 0.7 %shard_map.83 = (f32[24,8,32]{2,1,0:T(8,128)}, f32[24,2,32]{2,1,0:T(2,128)}) custom-call(f32[8,64,128]{2,1,0:T(8,128)S(1)} %all_to_all.10.parts), custom_call_target="tpu_custom_call" | custom-call | tf_op jit(solution)/shard_map/pallas_call | solution.py:724
  (1 shorter events, 0.0 us)
Async XLA Ops:
  0.6 17.0 %copy-start.2 = (s32[2,3]{1,0:T(2,128)S(1)}, s32[2,3]{1,0:T(2,128)}, u32[]{:S(2)}) copy-start(s32[2,3]{1,0:T(2,128)} %flags_in_hbm.1) | copy-start | bytes 76
  0.6 17.0 %copy-start.3 = (s32[2,2]{1,0:T(2,128)S(1)}, s32[2,2]{1,0:T(2,128)}, u32[]{:S(2)}) copy-start(s32[2,2]{1,0:T(2,128)} %param.8) | copy-start | bytes 52
  2.3 15.2 %all-to-all-start = ((f32[8,48,128]{2,1,0:T(8,128)}), f32[8,48,128]{2,1,0:T(8,128)S(1)}, u32[]{:S(2)}, u32[]{:S(2)}) async-start(f32[8,48,128]{2,1,0:T(8,128)} %shard_map.76), calls=%async_computation | async-start | bytes 393216 | tf_op jit(solution)/shard_map/all_to_all | solution.py:602
  17.6 1.4 %collective-permute-start = (f32[8,48,128]{2,1,0:T(8,128)S(1)}, f32[8,48,128]{2,1,0:T(8,128)S(1)}, u32[]{:S(2)}, u32[]{:S(2)}) collective-permute-start(f32[8,48,128]{2,1,0:T(8,128)S(1)} %all-to-all-done.near), channel_id=1, source_target_pairs={{0,2},{2,0},{4,6},{6,4},{8,10},{10,8},{12,14},{14,12},{16,18},{18,... | collective-permute-start | bytes 589832 | tf_op jit(solution)/shard_map/ppermute | solution.py:596
  19.0 5.7 %copy-start = (f32[2,4,192,256]{3,2,1,0:T(8,128)S(1)}, f32[2,4,192,256]{3,2,1,0:T(8,128)}, u32[]{:S(2)}) copy-start(f32[2,4,192,256]{3,2,1,0:T(8,128)} %get-tuple-element.21.moments) | copy-start | bytes 4718596
  21.0 4.9 %collective-permute-start.1 = (f32[12,8,256]{2,1,0:T(8,128)S(1)}, f32[12,8,256]{2,1,0:T(8,128)S(1)}, u32[]{:S(2)}, u32[]{:S(2)}) collective-permute-start(f32[12,8,256]{2,1,0:T(8,128)S(1)} %get-tuple-element.25.mine), channel_id=1, source_target_pairs={{0,1},{1,0},{2,3},{3,2},{4,5},{5,4},{6,7},{7,6},{8,9},{9,8},{10,11... | collective-permute-start | bytes 294920 | tf_op jit(solution)/shard_map/ppermute | solution.py:596
  22.6 3.3 %copy-start.1 = (bf16[2,12,8,256]{3,2,1,0:T(8,128)(2,1)S(1)}, bf16[2,12,8,256]{3,2,1,0:T(8,128)(2,1)}, u32[]{:S(2)}) copy-start(bf16[2,12,8,256]{3,2,1,0:T(8,128)(2,1)} %observed.3) | copy-start | bytes 294916
  24.1 4.7 %collective-permute-start.2 = (f32[12,8,256]{2,1,0:T(8,128)S(1)}, f32[12,8,256]{2,1,0:T(8,128)S(1)}, u32[]{:S(2)}, u32[]{:S(2)}) collective-permute-start(f32[12,8,256]{2,1,0:T(8,128)S(1)} %get-tuple-element.31.mine), channel_id=1, source_target_pairs={{0,1},{1,0},{2,3},{3,2},{4,5},{5,4},{6,7},{7,6},{8,9},{9,8},{10,11... | collective-permute-start | bytes 294920 | tf_op jit(solution)/shard_map/ppermute | solution.py:596
  30.7 1.6 %collective-permute-start.3 = (f32[8,64,128]{2,1,0:T(8,128)S(1)}, f32[8,64,128]{2,1,0:T(8,128)S(1)}, u32[]{:S(2)}, u32[]{:S(2)}) collective-permute-start(f32[8,64,128]{2,1,0:T(8,128)S(1)} %get-tuple-element.36), channel_id=1, source_target_pairs={{0,2},{2,0},{4,6},{6,4},{8,10},{10,8},{12,14},{14,12},{16,18},{18,... | collective-permute-start | bytes 786440 | tf_op jit(solution)/shard_map/ppermute | solution.py:596

commit v4 on v3

--- a/solution.py
+++ b/solution.py
@@ -542,9 +542,11 @@
     residual_before, residual_out, near, far, terms, residual, turned, semaphore,
     meta, meta_semaphore,
 ):
-    del residual_before, near_before, far_before
+    del residual_before
     meta_copy = pltpu.make_async_copy(meta_in_vmem, meta, meta_semaphore)
     meta_copy.start()
+    near[...] = near_before[...]
+    far[...] = far_before[...]
     sent = add_gradient_terms(
         tiles - 1, meta_in_vmem, masks, observed, mine, other, row_jones, col_jones, paired,
         residual_out, terms, residual, turned, semaphore,
@@ -716,7 +718,7 @@
         [slots, slots],
         scratch,
         [residual_shape],
-        {10: 0, 1: 1, 2: 2},
+        {10: 0},
     )
     parts = trade(near + swap_with(far, "tile", 1))
     directions, _, owned = jones.shape

time: 45.6 us -> 45.6 us (level)
  no operation moved by 1% of the time
where the time goes in v4:
time: 45.6 us; the launch traced here: 45.3 us
  Pallas kernels  15.5 us (34%)
  blocking collectives  12.2 us (27%)
  starting transfers between devices  9.52 us (21%)
  waiting for transfers between devices  7.18 us (16%)
  between operations  0.72 us (2%)
    pallas_call x7, Pallas kernels, call(): pl.pallas_call(kernel, in_specs=[place(space) for space in spaces], out_s...  14.7 us
    all_to_all x1, blocking collectives, trade(): lax.all_to_all(slots, 'tile', 0, 0, axis_index_groups=groups, tiled=True)  12.2 us
    all_to_all x1, starting transfers between devices, trade(): lax.all_to_all(slots, 'tile', 0, 0, axis_index_groups=groups, tiled=True)  7.29 us
    ppermute x4, waiting for transfers between devices, swap_with(): lax.ppermute(value, axis, [(place, place ^ mask) for place in range(size)])  3.91 us
    all_to_all x1, waiting for transfers between devices, trade(): lax.all_to_all(slots, 'tile', 0, 0, axis_index_groups=groups, tiled=True)  3.27 us
    ppermute x4, starting transfers between devices, swap_with(): lax.ppermute(value, axis, [(place, place ^ mask) for place in range(size)])  2.23 us
  transfers between devices with their start and end apart: 5, of which 5 were waited for; matrix products, arithmetic and copies ran while one was open for 0% of the time, Pallas kernels for 20%

profile of v4, /device:TPU:0, one launch (start us, length us, event | category | flops | bytes accessed | tf_op | source)
XLA Modules:
  0.0 45.3 jit_solution(17582254647042710010)
XLA Ops:
  0.6 0.0 copy-start.2
  0.6 0.0 copy-start.3
  0.7 1.7 %shard_map.76 = f32[8,48,128]{2,1,0:T(8,128)} custom-call(f32[24,8,32]{2,1,0:T(8,128)} %jones_in_hbm.1), custom_call_target="tpu_custom_call" | custom-call | tf_op jit(solution)/shard_map/pallas_call | solution.py:581
  2.3 7.3 %all-to-all-start = ((f32[8,48,128]{2,1,0:T(8,128)}), f32[8,48,128]{2,1,0:T(8,128)S(1)}, u32[]{:S(2)}, u32[]{:S(2)}) async-start(f32[8,48,128]{2,1,0:T(8,128)} %shard_map.76), calls=%async_computation | async-start | bytes 393216 | tf_op jit(solution)/shard_map/all_to_all | solution.py:604
  9.6 4.6 %shard_map.77 = (f32[2,4,192,256]{3,2,1,0:T(8,128)}, bf16[2,24,6,16,256]{4,3,2,1,0:T(8,128)(2,1)S(1)}) custom-call(s32[2,3]{1,0:T(2,128)} %flags_in_hbm.1, bf16[2,24,12,8,256]{4,3,2,1,0:T(8,128)(2,1)} %source.1), custom_call_target="tpu_custom_call" | custom-call | flops 11796480 | bytes 4718592 | tf_op jit(solution)/shard_map/pallas_call | solution.py:581
  14.2 0.1 pad_add_fusion.1
  14.3 3.3 %all-to-all-done.near = f32[8,48,128]{2,1,0:T(8,128)S(1)} async-done(((f32[8,48,128]{2,1,0:T(8,128)}), f32[8,48,128]{2,1,0:T(8,128)S(1)}, u32[]{:S(2)}, u32[]{:S(2)}) %all-to-all-start) | async-done | bytes 196640 | tf_op jit(solution)/shard_map/all_to_all | solution.py:604
  17.6 0.0 collective-permute-start
  17.6 0.0 copy-done.2
  17.6 0.0 copy-done.3
  17.6 0.1 pad_add_fusion.meta.meta_in_vmem
  17.7 1.4 %collective-permute-done.far = f32[8,48,128]{2,1,0:T(8,128)S(1)} collective-permute-done((f32[8,48,128]{2,1,0:T(8,128)S(1)}, f32[8,48,128]{2,1,0:T(8,128)S(1)}, u32[]{:S(2)}, u32[]{:S(2)}) %collective-permute-start) | collective-permute-done | bytes 196640 | tf_op jit(solution)/shard_map/ppermute | solution.py:598
  19.0 0.0 copy-start
  19.0 2.0 %shard_map.79 = (f32[12,8,256]{2,1,0:T(8,128)S(1)}, f32[2,2,200,128]{3,2,1,0:T(8,128)S(1)}, f32[2,2,200,128]{3,2,1,0:T(8,128)S(1)}, f32[24,6,2,8,256]{4,3,2,1,0:T(8,128)S(1)}) custom-call(s32[2,7]{1,0:T(2,128)S(1)} %pad_add_fusion.meta.meta_in_vmem, f32[8,48,128]{2,1,0:T(8,128)S(1)} %all-to-all-done.near, f32[8,48,128]{2,1,0:T(8,128)S(1)} %collective-permute-done.far, ...), custom_call_target="tpu_custom_call" | custom-call | tf_op jit(solution)/shard_map/pallas_call | solution.py:581
  21.0 1.6 %collective-permute-start.1 = (f32[12,8,256]{2,1,0:T(8,128)S(1)}, f32[12,8,256]{2,1,0:T(8,128)S(1)}, u32[]{:S(2)}, u32[]{:S(2)}) collective-permute-start(f32[12,8,256]{2,1,0:T(8,128)S(1)} %get-tuple-element.25.mine), channel_id=1, source_target_pairs={{0,1},{1,0},{2,3},{3,2},{4,5},{5,4},{6,7},{7,6},{8,9},{9,8},{10,11... | collective-permute-start | bytes 294920 | tf_op jit(solution)/shard_map/ppermute | solution.py:598
  22.6 0.0 copy-start.1
  22.6 1.5 %shard_map.81 = (f32[12,8,256]{2,1,0:T(8,128)S(1)}, f32[24,6,2,8,256]{4,3,2,1,0:T(8,128)S(1)}) custom-call(bf16[2,24,6,16,256]{4,3,2,1,0:T(8,128)(2,1)S(1)} %get-tuple-element.24.narrow, f32[2,2,200,128]{3,2,1,0:T(8,128)S(1)} %get-tuple-element.26.row_jones, f32[2,2,200,128]{3,2,1,0:T(8,128)S(1)} %get-tuple-element.27.col_jones), custom_call_target="tpu_custom_call" | custom-call | tf_op jit(solution)/shard_map/pallas_call | solution.py:581
  24.1 0.6 %collective-permute-start.2 = (f32[12,8,256]{2,1,0:T(8,128)S(1)}, f32[12,8,256]{2,1,0:T(8,128)S(1)}, u32[]{:S(2)}, u32[]{:S(2)}) collective-permute-start(f32[12,8,256]{2,1,0:T(8,128)S(1)} %get-tuple-element.31.mine), channel_id=1, source_target_pairs={{0,1},{1,0},{2,3},{3,2},{4,5},{5,4},{6,7},{7,6},{8,9},{9,8},{10,11... | collective-permute-start | bytes 294920 | tf_op jit(solution)/shard_map/ppermute | solution.py:598
  24.7 0.0 copy-done
  24.7 1.0 %shard_map.78 = (f32[2,2,48,256]{3,2,1,0:T(8,128)S(1)}, f32[2,4,8,256]{3,2,1,0:T(8,128)S(1)}) custom-call(s32[2,7]{1,0:T(2,128)S(1)} %pad_add_fusion.meta.meta_in_vmem, f32[8,48,128]{2,1,0:T(8,128)S(1)} %all-to-all-done.near, f32[8,48,128]{2,1,0:T(8,128)S(1)} %collective-permute-done.far, f32[2,4,192,256]{3,2,1,0:T(8,128)S(1)} %copy-done), custom_call_target="tpu_custom_call" | custom-call | flops 1179648 | bytes 1179648 | tf_op jit(solution)/shard_map/pallas_call | solution.py:581
  25.7 0.2 collective-permute-done.1.other
  25.9 0.0 copy-done.1
  25.9 2.0 %shard_map.80 = (f32[2,12,8,128]{3,2,1,0:T(8,128)}, f32[8,64,128]{2,1,0:T(8,128)S(1)}, f32[8,64,128]{2,1,0:T(8,128)S(1)}) custom-call(s32[2,7]{1,0:T(2,128)S(1)} %pad_add_fusion.meta.meta_in_vmem, f32[2,2,48,256]{3,2,1,0:T(8,128)S(1)} %get-tuple-element.22.curvature_terms, f32[2,4,8,256]{3,2,1,0:T(8,128)S(1)} %get-tuple-element.23.masks, ...), custom_call_target="tpu_custom_call" | custom-call | tf_op jit(solution)/shard_map/pallas_call | solution.py:581
  28.0 0.8 %collective-permute-done.2.other = f32[12,8,256]{2,1,0:T(8,128)S(1)} collective-permute-done((f32[12,8,256]{2,1,0:T(8,128)S(1)}, f32[12,8,256]{2,1,0:T(8,128)S(1)}, u32[]{:S(2)}, u32[]{:S(2)}) %collective-permute-start.2) | collective-permute-done | bytes 98336 | tf_op jit(solution)/shard_map/ppermute | solution.py:598
  28.8 2.0 %shard_map.82 = (f32[2,12,8,128]{3,2,1,0:T(8,128)}, f32[8,64,128]{2,1,0:T(8,128)S(1)}, f32[8,64,128]{2,1,0:T(8,128)S(1)}) custom-call(s32[2,7]{1,0:T(2,128)S(1)} %pad_add_fusion.meta.meta_in_vmem, f32[8,64,128]{2,1,0:T(8,128)S(1)} %get-tuple-element.29.near_before, f32[8,64,128]{2,1,0:T(8,128)S(1)} %get-tuple-element.30.far_before, ...), custom_call_target="tpu_custom_call", output_to_operand_aliasing={{0}: (10, {})} | custom-call | tf_op jit(solution)/shard_map/pallas_call | solution.py:581
  30.7 0.1 collective-permute-start.3
  30.8 1.5 %collective-permute-done.3 = f32[8,64,128]{2,1,0:T(8,128)S(1)} collective-permute-done((f32[8,64,128]{2,1,0:T(8,128)S(1)}, f32[8,64,128]{2,1,0:T(8,128)S(1)}, u32[]{:S(2)}, u32[]{:S(2)}) %collective-permute-start.3) | collective-permute-done | bytes 262176 | tf_op jit(solution)/shard_map/ppermute | solution.py:598
  32.4 12.2 %all_to_all.10.parts = f32[8,64,128]{2,1,0:T(8,128)S(1)} all-to-all(f32[8,64,128]{2,1,0:T(8,128)S(1)} %add.3), channel_id=1, replica_groups={{0,4,8,12,16,20,24,28},{2,6,10,14,18,22,26,30},{1,5,9,13,17,21,25,29},{..., dimensions={0} | all-to-all | bytes 524288 | tf_op jit(solution)/shard_map/all_to_all | solution.py:604
  44.5 0.7 %shard_map.83 = (f32[24,8,32]{2,1,0:T(8,128)}, f32[24,2,32]{2,1,0:T(2,128)}) custom-call(f32[8,64,128]{2,1,0:T(8,128)S(1)} %all_to_all.10.parts), custom_call_target="tpu_custom_call" | custom-call | tf_op jit(solution)/shard_map/pallas_call | solution.py:726
  (1 shorter events, 0.0 us)
Async XLA Ops:
  0.6 17.0 %copy-start.2 = (s32[2,3]{1,0:T(2,128)S(1)}, s32[2,3]{1,0:T(2,128)}, u32[]{:S(2)}) copy-start(s32[2,3]{1,0:T(2,128)} %flags_in_hbm.1) | copy-start | bytes 76
  0.6 17.0 %copy-start.3 = (s32[2,2]{1,0:T(2,128)S(1)}, s32[2,2]{1,0:T(2,128)}, u32[]{:S(2)}) copy-start(s32[2,2]{1,0:T(2,128)} %param.8) | copy-start | bytes 52
  2.3 15.2 %all-to-all-start = ((f32[8,48,128]{2,1,0:T(8,128)}), f32[8,48,128]{2,1,0:T(8,128)S(1)}, u32[]{:S(2)}, u32[]{:S(2)}) async-start(f32[8,48,128]{2,1,0:T(8,128)} %shard_map.76), calls=%async_computation | async-start | bytes 393216 | tf_op jit(solution)/shard_map/all_to_all | solution.py:604
  17.6 1.4 %collective-permute-start = (f32[8,48,128]{2,1,0:T(8,128)S(1)}, f32[8,48,128]{2,1,0:T(8,128)S(1)}, u32[]{:S(2)}, u32[]{:S(2)}) collective-permute-start(f32[8,48,128]{2,1,0:T(8,128)S(1)} %all-to-all-done.near), channel_id=1, source_target_pairs={{0,2},{2,0},{4,6},{6,4},{8,10},{10,8},{12,14},{14,12},{16,18},{18,... | collective-permute-start | bytes 589832 | tf_op jit(solution)/shard_map/ppermute | solution.py:598
  19.0 5.7 %copy-start = (f32[2,4,192,256]{3,2,1,0:T(8,128)S(1)}, f32[2,4,192,256]{3,2,1,0:T(8,128)}, u32[]{:S(2)}) copy-start(f32[2,4,192,256]{3,2,1,0:T(8,128)} %get-tuple-element.21.moments) | copy-start | bytes 4718596
  21.0 4.9 %collective-permute-start.1 = (f32[12,8,256]{2,1,0:T(8,128)S(1)}, f32[12,8,256]{2,1,0:T(8,128)S(1)}, u32[]{:S(2)}, u32[]{:S(2)}) collective-permute-start(f32[12,8,256]{2,1,0:T(8,128)S(1)} %get-tuple-element.25.mine), channel_id=1, source_target_pairs={{0,1},{1,0},{2,3},{3,2},{4,5},{5,4},{6,7},{7,6},{8,9},{9,8},{10,11... | collective-permute-start | bytes 294920 | tf_op jit(solution)/shard_map/ppermute | solution.py:598
  22.6 3.3 %copy-start.1 = (bf16[2,12,8,256]{3,2,1,0:T(8,128)(2,1)S(1)}, bf16[2,12,8,256]{3,2,1,0:T(8,128)(2,1)}, u32[]{:S(2)}) copy-start(bf16[2,12,8,256]{3,2,1,0:T(8,128)(2,1)} %observed.3) | copy-start | bytes 294916
  24.1 4.7 %collective-permute-start.2 = (f32[12,8,256]{2,1,0:T(8,128)S(1)}, f32[12,8,256]{2,1,0:T(8,128)S(1)}, u32[]{:S(2)}, u32[]{:S(2)}) collective-permute-start(f32[12,8,256]{2,1,0:T(8,128)S(1)} %get-tuple-element.31.mine), channel_id=1, source_target_pairs={{0,1},{1,0},{2,3},{3,2},{4,5},{5,4},{6,7},{7,6},{8,9},{9,8},{10,11... | collective-permute-start | bytes 294920 | tf_op jit(solution)/shard_map/ppermute | solution.py:598
  30.7 1.6 %collective-permute-start.3 = (f32[8,64,128]{2,1,0:T(8,128)S(1)}, f32[8,64,128]{2,1,0:T(8,128)S(1)}, u32[]{:S(2)}, u32[]{:S(2)}) collective-permute-start(f32[8,64,128]{2,1,0:T(8,128)S(1)} %get-tuple-element.36), channel_id=1, source_target_pairs={{0,2},{2,0},{4,6},{6,4},{8,10},{10,8},{12,14},{14,12},{16,18},{18,... | collective-permute-start | bytes 786440 | tf_op jit(solution)/shard_map/ppermute | solution.py:598

commit v5 on v4

--- a/solution.py
+++ b/solution.py
@@ -273,7 +273,7 @@
 
         for n, copy in enumerate(copies[tile]):
             copy.wait()
-            lax.fori_loop(n * each, (n + 1) * each, add_direction, 0)
+            lax.fori_loop(n * each, (n + 1) * each, add_direction, 0, unroll=2)
             rows = pl.ds(8 * n * each, 8 * each)
             sent.append(
                 pltpu.make_async_copy(

time: 45.6 us -> 45.6 us (level)
  no operation moved by 1% of the time
where the time goes in v5:
time: 45.6 us; the launch traced here: 45.3 us
  Pallas kernels  15.2 us (33%)
  blocking collectives  12.2 us (27%)
  starting transfers between devices  9.52 us (21%)
  waiting for transfers between devices  7.42 us (16%)
  between operations  0.72 us (2%)
    pallas_call x7, Pallas kernels, call(): pl.pallas_call(kernel, in_specs=[place(space) for space in spaces], out_s...  14.5 us
    all_to_all x1, blocking collectives, trade(): lax.all_to_all(slots, 'tile', 0, 0, axis_index_groups=groups, tiled=True)  12.2 us
    all_to_all x1, starting transfers between devices, trade(): lax.all_to_all(slots, 'tile', 0, 0, axis_index_groups=groups, tiled=True)  7.29 us
    ppermute x4, waiting for transfers between devices, swap_with(): lax.ppermute(value, axis, [(place, place ^ mask) for place in range(size)])  3.91 us
    all_to_all x1, waiting for transfers between devices, trade(): lax.all_to_all(slots, 'tile', 0, 0, axis_index_groups=groups, tiled=True)  3.51 us
    ppermute x4, starting transfers between devices, swap_with(): lax.ppermute(value, axis, [(place, place ^ mask) for place in range(size)])  2.23 us
  transfers between devices with their start and end apart: 5, of which 5 were waited for; matrix products, arithmetic and copies ran while one was open for 0% of the time, Pallas kernels for 20%

profile of v5, /device:TPU:0, one launch (start us, length us, event | category | flops | bytes accessed | tf_op | source)
XLA Modules:
  0.0 45.3 jit_solution(2710306704238413259)
XLA Ops:
  0.6 0.0 copy-start.2
  0.6 0.0 copy-start.3
  0.7 1.7 %shard_map.76 = f32[8,48,128]{2,1,0:T(8,128)} custom-call(f32[24,8,32]{2,1,0:T(8,128)} %jones_in_hbm.1), custom_call_target="tpu_custom_call" | custom-call | tf_op jit(solution)/shard_map/pallas_call | solution.py:581
  2.3 7.3 %all-to-all-start = ((f32[8,48,128]{2,1,0:T(8,128)}), f32[8,48,128]{2,1,0:T(8,128)S(1)}, u32[]{:S(2)}, u32[]{:S(2)}) async-start(f32[8,48,128]{2,1,0:T(8,128)} %shard_map.76), calls=%async_computation | async-start | bytes 393216 | tf_op jit(solution)/shard_map/all_to_all | solution.py:604
  9.6 4.4 %shard_map.77 = (f32[2,4,192,256]{3,2,1,0:T(8,128)}, bf16[2,24,6,16,256]{4,3,2,1,0:T(8,128)(2,1)S(1)}) custom-call(s32[2,3]{1,0:T(2,128)} %flags_in_hbm.1, bf16[2,24,12,8,256]{4,3,2,1,0:T(8,128)(2,1)} %source.1), custom_call_target="tpu_custom_call" | custom-call | flops 11796480 | bytes 4718592 | tf_op jit(solution)/shard_map/pallas_call | solution.py:581
  14.0 0.1 pad_add_fusion.1
  14.1 3.5 %all-to-all-done.near = f32[8,48,128]{2,1,0:T(8,128)S(1)} async-done(((f32[8,48,128]{2,1,0:T(8,128)}), f32[8,48,128]{2,1,0:T(8,128)S(1)}, u32[]{:S(2)}, u32[]{:S(2)}) %all-to-all-start) | async-done | bytes 196640 | tf_op jit(solution)/shard_map/all_to_all | solution.py:604
  17.6 0.0 collective-permute-start
  17.6 0.0 copy-done.2
  17.6 0.0 copy-done.3
  17.6 0.1 pad_add_fusion.meta.meta_in_vmem
  17.7 1.4 %collective-permute-done.far = f32[8,48,128]{2,1,0:T(8,128)S(1)} collective-permute-done((f32[8,48,128]{2,1,0:T(8,128)S(1)}, f32[8,48,128]{2,1,0:T(8,128)S(1)}, u32[]{:S(2)}, u32[]{:S(2)}) %collective-permute-start) | collective-permute-done | bytes 196640 | tf_op jit(solution)/shard_map/ppermute | solution.py:598
  19.0 0.0 copy-start
  19.0 2.0 %shard_map.79 = (f32[12,8,256]{2,1,0:T(8,128)S(1)}, f32[2,2,200,128]{3,2,1,0:T(8,128)S(1)}, f32[2,2,200,128]{3,2,1,0:T(8,128)S(1)}, f32[24,6,2,8,256]{4,3,2,1,0:T(8,128)S(1)}) custom-call(s32[2,7]{1,0:T(2,128)S(1)} %pad_add_fusion.meta.meta_in_vmem, f32[8,48,128]{2,1,0:T(8,128)S(1)} %all-to-all-done.near, f32[8,48,128]{2,1,0:T(8,128)S(1)} %collective-permute-done.far, ...), custom_call_target="tpu_custom_call" | custom-call | tf_op jit(solution)/shard_map/pallas_call | solution.py:581
  21.0 1.6 %collective-permute-start.1 = (f32[12,8,256]{2,1,0:T(8,128)S(1)}, f32[12,8,256]{2,1,0:T(8,128)S(1)}, u32[]{:S(2)}, u32[]{:S(2)}) collective-permute-start(f32[12,8,256]{2,1,0:T(8,128)S(1)} %get-tuple-element.25.mine), channel_id=1, source_target_pairs={{0,1},{1,0},{2,3},{3,2},{4,5},{5,4},{6,7},{7,6},{8,9},{9,8},{10,11... | collective-permute-start | bytes 294920 | tf_op jit(solution)/shard_map/ppermute | solution.py:598
  22.6 0.0 copy-start.1
  22.6 1.5 %shard_map.81 = (f32[12,8,256]{2,1,0:T(8,128)S(1)}, f32[24,6,2,8,256]{4,3,2,1,0:T(8,128)S(1)}) custom-call(bf16[2,24,6,16,256]{4,3,2,1,0:T(8,128)(2,1)S(1)} %get-tuple-element.24.narrow, f32[2,2,200,128]{3,2,1,0:T(8,128)S(1)} %get-tuple-element.26.row_jones, f32[2,2,200,128]{3,2,1,0:T(8,128)S(1)} %get-tuple-element.27.col_jones), custom_call_target="tpu_custom_call" | custom-call | tf_op jit(solution)/shard_map/pallas_call | solution.py:581
  24.1 0.6 %collective-permute-start.2 = (f32[12,8,256]{2,1,0:T(8,128)S(1)}, f32[12,8,256]{2,1,0:T(8,128)S(1)}, u32[]{:S(2)}, u32[]{:S(2)}) collective-permute-start(f32[12,8,256]{2,1,0:T(8,128)S(1)} %get-tuple-element.31.mine), channel_id=1, source_target_pairs={{0,1},{1,0},{2,3},{3,2},{4,5},{5,4},{6,7},{7,6},{8,9},{9,8},{10,11... | collective-permute-start | bytes 294920 | tf_op jit(solution)/shard_map/ppermute | solution.py:598
  24.7 0.0 copy-done
  24.7 1.0 %shard_map.78 = (f32[2,2,48,256]{3,2,1,0:T(8,128)S(1)}, f32[2,4,8,256]{3,2,1,0:T(8,128)S(1)}) custom-call(s32[2,7]{1,0:T(2,128)S(1)} %pad_add_fusion.meta.meta_in_vmem, f32[8,48,128]{2,1,0:T(8,128)S(1)} %all-to-all-done.near, f32[8,48,128]{2,1,0:T(8,128)S(1)} %collective-permute-done.far, f32[2,4,192,256]{3,2,1,0:T(8,128)S(1)} %copy-done), custom_call_target="tpu_custom_call" | custom-call | flops 1179648 | bytes 1179648 | tf_op jit(solution)/shard_map/pallas_call | solution.py:581
  25.7 0.2 collective-permute-done.1.other
  25.9 0.0 copy-done.1
  25.9 2.0 %shard_map.80 = (f32[2,12,8,128]{3,2,1,0:T(8,128)}, f32[8,64,128]{2,1,0:T(8,128)S(1)}, f32[8,64,128]{2,1,0:T(8,128)S(1)}) custom-call(s32[2,7]{1,0:T(2,128)S(1)} %pad_add_fusion.meta.meta_in_vmem, f32[2,2,48,256]{3,2,1,0:T(8,128)S(1)} %get-tuple-element.22.curvature_terms, f32[2,4,8,256]{3,2,1,0:T(8,128)S(1)} %get-tuple-element.23.masks, ...), custom_call_target="tpu_custom_call" | custom-call | tf_op jit(solution)/shard_map/pallas_call | solution.py:581
  28.0 0.8 %collective-permute-done.2.other = f32[12,8,256]{2,1,0:T(8,128)S(1)} collective-permute-done((f32[12,8,256]{2,1,0:T(8,128)S(1)}, f32[12,8,256]{2,1,0:T(8,128)S(1)}, u32[]{:S(2)}, u32[]{:S(2)}) %collective-permute-start.2) | collective-permute-done | bytes 98336 | tf_op jit(solution)/shard_map/ppermute | solution.py:598
  28.8 2.0 %shard_map.82 = (f32[2,12,8,128]{3,2,1,0:T(8,128)}, f32[8,64,128]{2,1,0:T(8,128)S(1)}, f32[8,64,128]{2,1,0:T(8,128)S(1)}) custom-call(s32[2,7]{1,0:T(2,128)S(1)} %pad_add_fusion.meta.meta_in_vmem, f32[8,64,128]{2,1,0:T(8,128)S(1)} %get-tuple-element.29.near_before, f32[8,64,128]{2,1,0:T(8,128)S(1)} %get-tuple-element.30.far_before, ...), custom_call_target="tpu_custom_call", output_to_operand_aliasing={{0}: (10, {})} | custom-call | tf_op jit(solution)/shard_map/pallas_call | solution.py:581
  30.7 0.1 collective-permute-start.3
  30.8 1.5 %collective-permute-done.3 = f32[8,64,128]{2,1,0:T(8,128)S(1)} collective-permute-done((f32[8,64,128]{2,1,0:T(8,128)S(1)}, f32[8,64,128]{2,1,0:T(8,128)S(1)}, u32[]{:S(2)}, u32[]{:S(2)}) %collective-permute-start.3) | collective-permute-done | bytes 262176 | tf_op jit(solution)/shard_map/ppermute | solution.py:598
  32.4 12.2 %all_to_all.10.parts = f32[8,64,128]{2,1,0:T(8,128)S(1)} all-to-all(f32[8,64,128]{2,1,0:T(8,128)S(1)} %add.3), channel_id=1, replica_groups={{0,4,8,12,16,20,24,28},{2,6,10,14,18,22,26,30},{1,5,9,13,17,21,25,29},{..., dimensions={0} | all-to-all | bytes 524288 | tf_op jit(solution)/shard_map/all_to_all | solution.py:604
  44.5 0.7 %shard_map.83 = (f32[24,8,32]{2,1,0:T(8,128)}, f32[24,2,32]{2,1,0:T(2,128)}) custom-call(f32[8,64,128]{2,1,0:T(8,128)S(1)} %all_to_all.10.parts), custom_call_target="tpu_custom_call" | custom-call | tf_op jit(solution)/shard_map/pallas_call | solution.py:726
  (1 shorter events, 0.0 us)
Async XLA Ops:
  0.6 17.0 %copy-start.2 = (s32[2,3]{1,0:T(2,128)S(1)}, s32[2,3]{1,0:T(2,128)}, u32[]{:S(2)}) copy-start(s32[2,3]{1,0:T(2,128)} %flags_in_hbm.1) | copy-start | bytes 76
  0.6 17.0 %copy-start.3 = (s32[2,2]{1,0:T(2,128)S(1)}, s32[2,2]{1,0:T(2,128)}, u32[]{:S(2)}) copy-start(s32[2,2]{1,0:T(2,128)} %param.8) | copy-start | bytes 52
  2.3 15.2 %all-to-all-start = ((f32[8,48,128]{2,1,0:T(8,128)}), f32[8,48,128]{2,1,0:T(8,128)S(1)}, u32[]{:S(2)}, u32[]{:S(2)}) async-start(f32[8,48,128]{2,1,0:T(8,128)} %shard_map.76), calls=%async_computation | async-start | bytes 393216 | tf_op jit(solution)/shard_map/all_to_all | solution.py:604
  17.6 1.4 %collective-permute-start = (f32[8,48,128]{2,1,0:T(8,128)S(1)}, f32[8,48,128]{2,1,0:T(8,128)S(1)}, u32[]{:S(2)}, u32[]{:S(2)}) collective-permute-start(f32[8,48,128]{2,1,0:T(8,128)S(1)} %all-to-all-done.near), channel_id=1, source_target_pairs={{0,2},{2,0},{4,6},{6,4},{8,10},{10,8},{12,14},{14,12},{16,18},{18,... | collective-permute-start | bytes 589832 | tf_op jit(solution)/shard_map/ppermute | solution.py:598
  19.0 5.7 %copy-start = (f32[2,4,192,256]{3,2,1,0:T(8,128)S(1)}, f32[2,4,192,256]{3,2,1,0:T(8,128)}, u32[]{:S(2)}) copy-start(f32[2,4,192,256]{3,2,1,0:T(8,128)} %get-tuple-element.21.moments) | copy-start | bytes 4718596
  21.0 4.9 %collective-permute-start.1 = (f32[12,8,256]{2,1,0:T(8,128)S(1)}, f32[12,8,256]{2,1,0:T(8,128)S(1)}, u32[]{:S(2)}, u32[]{:S(2)}) collective-permute-start(f32[12,8,256]{2,1,0:T(8,128)S(1)} %get-tuple-element.25.mine), channel_id=1, source_target_pairs={{0,1},{1,0},{2,3},{3,2},{4,5},{5,4},{6,7},{7,6},{8,9},{9,8},{10,11... | collective-permute-start | bytes 294920 | tf_op jit(solution)/shard_map/ppermute | solution.py:598
  22.6 3.3 %copy-start.1 = (bf16[2,12,8,256]{3,2,1,0:T(8,128)(2,1)S(1)}, bf16[2,12,8,256]{3,2,1,0:T(8,128)(2,1)}, u32[]{:S(2)}) copy-start(bf16[2,12,8,256]{3,2,1,0:T(8,128)(2,1)} %observed.3) | copy-start | bytes 294916
  24.1 4.7 %collective-permute-start.2 = (f32[12,8,256]{2,1,0:T(8,128)S(1)}, f32[12,8,256]{2,1,0:T(8,128)S(1)}, u32[]{:S(2)}, u32[]{:S(2)}) collective-permute-start(f32[12,8,256]{2,1,0:T(8,128)S(1)} %get-tuple-element.31.mine), channel_id=1, source_target_pairs={{0,1},{1,0},{2,3},{3,2},{4,5},{5,4},{6,7},{7,6},{8,9},{9,8},{10,11... | collective-permute-start | bytes 294920 | tf_op jit(solution)/shard_map/ppermute | solution.py:598
  30.7 1.6 %collective-permute-start.3 = (f32[8,64,128]{2,1,0:T(8,128)S(1)}, f32[8,64,128]{2,1,0:T(8,128)S(1)}, u32[]{:S(2)}, u32[]{:S(2)}) collective-permute-start(f32[8,64,128]{2,1,0:T(8,128)S(1)} %get-tuple-element.36), channel_id=1, source_target_pairs={{0,2},{2,0},{4,6},{6,4},{8,10},{10,8},{12,14},{14,12},{16,18},{18,... | collective-permute-start | bytes 786440 | tf_op jit(solution)/shard_map/ppermute | solution.py:598
